TPU v7x, 1024 devices: a whole 8x8x8 slice. The times are simulated.
1024 devices in a mesh: seq: 16 (over y, core), exp: 16 (over x_lo, z), rep: 4 (over x_hi).
Axes of the slice: x: 8 (x_hi: 4, x_lo: 2; x = x_hi * 2 + x_lo), y: 8, z: 8, core: 2. Of those that a mesh axis runs over, the one named last changes fastest.
Arguments:
- queries: bfloat16 [2048, 6144], P('seq'), may hold values from -80 to 80
- keys: bfloat16 [2048, 1024], P('seq'), may hold values from -4.2 to 4.2
- values: bfloat16 [2048, 1024], P('seq'), may hold values from -6.2 to 6.2
- lengths: int32 [16], replicated, may hold values from 1 to 256, 2048 in all
- expert_ids: int32 [2048, 4], P('seq'), may hold values from 0 to 15, all different within a row; in each aligned block of 128 rows (0 to 127, 128 to 255, ...) at most 34 rows name the same one
- gate_share: float32 [2048, 4], P('seq'), may hold values from 0.2 to 1
- gate_up: bfloat16 [16, 6144, 2, 5376], P('exp', 'rep', None, 'seq'), may hold values from -0.15625 to 0.15625
- down_t: bfloat16 [16, 6144, 5376], P('exp', 'rep', 'seq'), may hold values from -0.15625 to 0.15625
Outputs:
- moe_out: bfloat16 [2048, 6144], P(('seq', 'exp'), 'rep')
Inputs may be any that keep to these rules, and one draw needn't show every extreme that they name: The lengths sum to 2048; each is at most 256, and one is exactly 256. `expert_ids`: each token names 4 different experts. Among the 128 tokens of one device (aligned blocks of 128 positions), no expert is named more than 34 times, a bound that some block reaches.
All inputs are finite; a program needn't handle non-finite values.
Results may differ from a plain program's by a relative error of at most 0.035.
Values may be sent and summed in bfloat16 or wider, within the bound.
No kernel may reach another device: no remote copies, remote signals or barrier semaphores. Data moves between devices by JAX's collectives and lax.ppermute only.
A program may use at most 64 MiB of HBM per device.

v0:
```python
import jax
import jax.numpy as jnp
from jax import lax
from jax.sharding import PartitionSpec as P

HEADS = 48
KV = 8
HD = 128
TOPK = 4
REACH = 2
CAP = 34


def segment_ids(lens, length):
    ends = jnp.cumsum(lens)
    places = jnp.arange(length, dtype=jnp.int32)
    return jnp.sum((places[:, None] >= ends[None, :]).astype(jnp.int32), axis=1)


def softmax_rows(scores):
    top = jnp.max(scores, axis=-1, keepdims=True)
    weights = jnp.exp(scores - top)
    return (weights / jnp.sum(weights, axis=-1, keepdims=True)).astype(jnp.bfloat16)


def earlier(blocks_arr, back, fill):
    padding = jnp.full((back,) + blocks_arr.shape[1:], fill, blocks_arr.dtype)
    return jnp.concatenate([padding, blocks_arr[: blocks_arr.shape[0] - back]], 0)


def widen(blocks_arr, fill):
    parts = [earlier(blocks_arr, back, fill) for back in range(REACH, 0, -1)]
    return jnp.concatenate(parts + [blocks_arr], 1)


def per_device(queries, keys, values, lengths, expert_ids, gate_share, gate_up, down_t):
    n_seq = lax.axis_size("seq")
    tok = queries.shape[0]
    length = tok * n_seq
    owned = gate_up.shape[0]
    cols = gate_up.shape[1]
    rep_index = lax.axis_index("rep")
    segment = segment_ids(lengths, length)
    local_heads = HEADS // n_seq
    repeat = max(1, n_seq // KV)
    slots = KV * repeat // n_seq
    per_slot = local_heads // slots
    q_send = queries.reshape(tok, n_seq, local_heads * HD)
    kv_rows = jnp.concatenate([keys.reshape(tok, KV, HD), values.reshape(tok, KV, HD)], axis=2)
    kv_send = jnp.repeat(kv_rows, repeat, axis=1)
    q_all, kv_all = (
        lax.all_to_all(q_send, "seq", split_axis=1, concat_axis=0, tiled=True),
        lax.all_to_all(kv_send, "seq", split_axis=1, concat_axis=0, tiled=True),
    )
    q_tile = q_all.reshape(n_seq, tok, slots, per_slot, HD)
    kv_wide = widen(kv_all.reshape(n_seq, tok, slots, 2 * HD), 0)
    seg_tile = segment.reshape(n_seq, tok)
    seg_keys = widen(seg_tile, -1)
    q_pos = jnp.arange(length, dtype=jnp.int32).reshape(n_seq, tok)
    k_pos = q_pos[:, :1] - REACH * tok + jnp.arange((REACH + 1) * tok, dtype=jnp.int32)[None, :]
    allowed = (seg_tile[:, :, None] == seg_keys[:, None, :]) & (
        k_pos[:, None, :] <= q_pos[:, :, None]
    )

    def one_head(q_head):
        scores = jnp.einsum(
            "ntsd,nksd->nstk", q_head, kv_wide[..., :HD], preferred_element_type=jnp.float32
        ) * HD ** (-0.5)
        scores = jnp.where(allowed[:, None], scores, -jnp.inf)
        probs = softmax_rows(scores)
        mixed_rows = jnp.einsum(
            "nstk,nksd->ntsd", probs, kv_wide[..., HD:], preferred_element_type=jnp.float32
        )
        return mixed_rows.astype(jnp.bfloat16)

    result = lax.map(one_head, jnp.moveaxis(q_tile, 3, 0))
    result = jnp.moveaxis(result, 0, 3).reshape(length, local_heads * HD)
    attended = lax.all_to_all(result, "seq", split_axis=0, concat_axis=1, tiled=True)
    local_cols = lax.dynamic_slice_in_dim(attended, rep_index * cols, cols, 1)
    routes = tok * TOPK
    mine = lax.axis_index("exp") * owned + jnp.arange(owned, dtype=jnp.int32)
    ids = expert_ids.reshape(routes)
    shares = gate_share.reshape(routes)
    match = (ids[None, :] == mine[:, None]).astype(jnp.int32)
    rank = jnp.cumsum(match, axis=1) - match
    slot_hit = match[:, None, :] * (
        rank[:, None, :] == jnp.arange(CAP, dtype=jnp.int32)[None, :, None]
    ).astype(jnp.int32)
    token_of = jnp.arange(routes, dtype=jnp.int32) // TOPK
    token_for = jnp.sum(slot_hit * token_of[None, None, :], axis=2)
    live = jnp.sum(slot_hit, axis=2)
    share_for = jnp.sum(slot_hit.astype(jnp.float32) * shares[None, None, :], axis=2)
    picked = local_cols[token_for] * live[..., None].astype(jnp.bfloat16)
    both_part = jnp.einsum(
        "ecd,edgf->ecgf",
        lax.all_gather(picked, "seq", axis=1, tiled=True),
        gate_up,
        preferred_element_type=jnp.float32,
    )
    both_part = lax.optimization_barrier(both_part.astype(jnp.bfloat16)).astype(jnp.float32)
    both = lax.psum(both_part.astype(jnp.bfloat16), "rep").astype(jnp.float32)
    hidden = (jax.nn.silu(both[:, :, 0]) * both[:, :, 1]).astype(jnp.bfloat16)
    down_part = jnp.einsum("ecf,edf->ecd", hidden, down_t, preferred_element_type=jnp.float32)
    down_part = lax.optimization_barrier(down_part.astype(jnp.bfloat16)).astype(jnp.float32)
    expert_out = lax.psum_scatter(
        down_part.astype(jnp.bfloat16), "seq", scatter_dimension=1, tiled=True
    ).astype(jnp.float32)
    weighted = expert_out * (live.astype(jnp.float32) * share_for)[..., None]
    term = jax.ops.segment_sum(
        weighted.reshape(owned * CAP, cols), token_for.reshape(owned * CAP), num_segments=tok
    )
    term = lax.optimization_barrier(term.astype(jnp.bfloat16)).astype(jnp.float32)
    mixed = lax.psum_scatter(term.astype(jnp.bfloat16), "exp", scatter_dimension=0, tiled=True)
    return mixed


def solution(mesh):
    in_specs = (
        P("seq", None),
        P("seq", None),
        P("seq", None),
        P(),
        P("seq", None),
        P("seq", None),
        P("exp", "rep", None, "seq"),
        P("exp", "rep", "seq"),
    )
    out_specs = P(("seq", "exp"), "rep")
    return jax.shard_map(
        per_device, mesh=mesh, in_specs=in_specs, out_specs=out_specs, check_vma=False
    )
```

profile of v0, /device:TPU:14, one launch (start us, length us, event | category | flops | bytes accessed | tf_op | source)
XLA Modules:
  0.0 423.3 jit_solution(12567093997682549503)
XLA Ops:
  10.0 7.7 %all-to-all-start.1 = ((bf16[128,16,256]{2,0,1:T(8,128)(2,1)}), bf16[128,16,256]{2,0,1:T(8,128)(2,1)S(1)}, u32[]{:S(2)}, u32[]{:S(2)}) async-start(bf16[128,16,256]{2,0,1:T(8,128)(2,1)} %bitcast.130), calls=%async_computation.1 | async-start | bytes 2097152 | tf_op jit(solution)/shard_map/all_to_all | solution.py:53
  17.6 2.6 copy.42
  20.2 24.1 %all-to-all-done.1 = bf16[128,16,256]{2,0,1:T(8,128)(2,1)S(1)} async-done(((bf16[128,16,256]{2,0,1:T(8,128)(2,1)}), bf16[128,16,256]{2,0,1:T(8,128)(2,1)S(1)}, u32[]{:S(2)}, u32[]{:S(2)}) %all-to-all-start.1) | async-done | bytes 1048608 | tf_op jit(solution)/shard_map/all_to_all | solution.py:53
  44.3 4.8 %all-to-all-start = ((bf16[128,16,384]{0,2,1:T(8,128)(2,1)}), bf16[128,16,384]{0,2,1:T(8,128)(2,1)}, u32[]{:S(2)}, u32[]{:S(2)}) async-start(bf16[128,16,384]{0,2,1:T(8,128)(2,1)} %bitcast.129), calls=%async_computation | async-start | bytes 3145728 | tf_op jit(solution)/shard_map/all_to_all | solution.py:52
  49.9 1.9 fusion.46
  51.8 35.2 %all-to-all-done = bf16[128,16,384]{0,2,1:T(8,128)(2,1)} async-done(((bf16[128,16,384]{0,2,1:T(8,128)(2,1)}), bf16[128,16,384]{0,2,1:T(8,128)(2,1)}, u32[]{:S(2)}, u32[]{:S(2)}) %all-to-all-start) | async-done | bytes 1572896 | tf_op jit(solution)/shard_map/all_to_all | solution.py:52
  87.0 25.4 %while.11 = (s32[]{:T(128)}, bf16[3,16,128,1,128]{2,4,0,1,3:T(8,128)(2,1)}, bf16[3,16,128,1,128]{2,4,0,1,3:T(8,128)(2,1)}, bf16[16,384,1,256]{3,1,0,2:T(8,128)(2...) while((s32[]{:T(128)}, ...), condition=%wide.region_8.9_spmd.clone, body=%wide.region_5.8_spmd.clone.sunk | while | flops 409993600 | bytes 12665949 | solution.py:76
  87.0 4.3 %fusion.97 = (f32[16,128]{1,0:T(8,128)S(1)}, f32[16,128,384]{2,1,0:T(8,128)}) fusion(s32[16,128]{1,0:T(8,128)S(1)} %get-tuple-element.188, s32[16,384]{1,0:T(8,128)S(1)} %get-tuple-element.189, s32[16,384]{1,0:T(8,128)S(1)} %get-tuple-element.186, s32[16,128]{1,0:T(8,128)S(1)} %get-tuple-element.187, ...), kind=kOutput, calls=%fused_computation.95.clone.1 | convolution fusion | flops 206832000 | bytes 5317120 | tf_op jit(solution)/shard_map/while/body/eval_jaxpr/sub | solution.py:22
  91.3 3.0 fusion.98
  95.5 4.3 %fusion.97 = (f32[16,128]{1,0:T(8,128)S(1)}, f32[16,128,384]{2,1,0:T(8,128)}) fusion(s32[16,128]{1,0:T(8,128)S(1)} %get-tuple-element.188, s32[16,384]{1,0:T(8,128)S(1)} %get-tuple-element.189, s32[16,384]{1,0:T(8,128)S(1)} %get-tuple-element.186, s32[16,128]{1,0:T(8,128)S(1)} %get-tuple-element.187, ...), kind=kOutput, calls=%fused_computation.95.clone.1 | convolution fusion | flops 206832000 | bytes 5317120 | tf_op jit(solution)/shard_map/while/body/eval_jaxpr/sub | solution.py:22
  99.8 3.0 fusion.98
  104.0 4.3 %fusion.97 = (f32[16,128]{1,0:T(8,128)S(1)}, f32[16,128,384]{2,1,0:T(8,128)}) fusion(s32[16,128]{1,0:T(8,128)S(1)} %get-tuple-element.188, s32[16,384]{1,0:T(8,128)S(1)} %get-tuple-element.189, s32[16,384]{1,0:T(8,128)S(1)} %get-tuple-element.186, s32[16,128]{1,0:T(8,128)S(1)} %get-tuple-element.187, ...), kind=kOutput, calls=%fused_computation.95.clone.1 | convolution fusion | flops 206832000 | bytes 5317120 | tf_op jit(solution)/shard_map/while/body/eval_jaxpr/sub | solution.py:22
  108.3 3.0 fusion.98
  112.4 5.0 %all-to-all-start.2 = ((bf16[16,128,384]{1,2,0:T(8,128)(2,1)}), bf16[16,128,384]{1,2,0:T(8,128)(2,1)}, u32[]{:S(2)}, u32[]{:S(2)}) async-start(bf16[16,128,384]{1,2,0:T(8,128)(2,1)} %bitcast.131), calls=%async_computation.2 | async-start | bytes 3145728 | tf_op jit(solution)/shard_map/all_to_all | solution.py:78
  118.7 1.3 fusion.83
  120.0 35.4 %all-to-all-done.2 = bf16[16,128,384]{1,2,0:T(8,128)(2,1)} async-done(((bf16[16,128,384]{1,2,0:T(8,128)(2,1)}), bf16[16,128,384]{1,2,0:T(8,128)(2,1)}, u32[]{:S(2)}, u32[]{:S(2)}) %all-to-all-start.2) | async-done | bytes 1572896 | tf_op jit(solution)/shard_map/all_to_all | solution.py:78
  158.3 54.7 %all-gather.2.cloned.1.call-done = bf16[1,544,1536]{2,0,1:T(2,128)(2,1)} async-done(((bf16[1,34,1536]{2,0,1:T(2,128)(2,1)}), bf16[1,544,1536]{2,0,1:T(2,128)(2,1)}) %all-gather.2.cloned.1.call-update) | async-done | bytes 1671184 | tf_op jit(solution)/shard_map/all_gather | solution.py:96
  213.0 4.4 %fusion.57 = bf16[1,544,2,336]{3,1,2,0:T(8,128)(2,1)} fusion(bf16[1,1536,2,336]{1,3,2,0:T(8,128)(2,1)S(1)} %copy-done, bf16[1,544,1536]{2,0,1:T(2,128)(2,1)} %all-gather.2.cloned.1.call-done), kind=kOutput, calls=%fused_computation.44 | convolution fusion | flops 1123390464 | bytes 4466688 | tf_op jit(solution)/shard_map/ecd,edgf->ecgf/dot_general | solution.py:94
  218.0 72.3 %all-reduce.8.cloned.1.call-done = bf16[1,544,2,336]{3,1,2,0:T(8,128)(2,1)} async-done(((bf16[1,544,2,336]{3,1,2,0:T(8,128)(2,1)}), bf16[1,544,2,336]{3,1,2,0:T(8,128)(2,1)}) %all-reduce.8.cloned.1.call-update) | async-done | bytes 731152 | tf_op jit(solution)/shard_map/psum | solution.py:101
  291.6 3.5 fusion.47
  295.1 32.6 %fusion.2 = bf16[40,1536]{1,0:T(8,128)(2,1)S(1)} fusion(bf16[1,544,1536]{2,1,0:T(8,128)(2,1)} %fusion.47), kind=kCustom, calls=%all-reduce-scatter | all-reduce-scatter fusion | flops 983041 | bytes 1798144
  327.7 1.3 collective-permute-start
  330.3 2.4 collective-permute-start.2
  337.3 79.4 %reduce-scatter.5.cloned.1.call-done = bf16[8,1536]{1,0:T(8,128)(2,1)} async-done(((bf16[128,1536]{1,0:T(8,128)(2,1)}), bf16[8,1536]{1,0:T(8,128)(2,1)}) %reduce-scatter.5.cloned.1.call-update) | async-done | bytes 24592 | tf_op jit(solution)/shard_map/reduce_scatter | solution.py:113
  (69 shorter events, 18.7 us)
Async XLA Ops:
  6.5 206.5 %copy-start = (bf16[1,1536,2,336]{1,3,2,0:T(8,128)(2,1)S(1)}, bf16[1,1536,2,336]{1,3,2,0:T(8,128)(2,1)}, u32[]{:S(2)}) copy-start(bf16[1,1536,2,336]{1,3,2,0:T(8,128)(2,1)} %param.16) | copy-start | bytes 6193156
  10.0 34.3 %all-to-all-start.1 = ((bf16[128,16,256]{2,0,1:T(8,128)(2,1)}), bf16[128,16,256]{2,0,1:T(8,128)(2,1)S(1)}, u32[]{:S(2)}, u32[]{:S(2)}) async-start(bf16[128,16,256]{2,0,1:T(8,128)(2,1)} %bitcast.130), calls=%async_computation.1 | async-start | bytes 2097152 | tf_op jit(solution)/shard_map/all_to_all | solution.py:53
  17.6 31.5 %copy-start.3 = (s32[16]{0:T(128)S(1)}, s32[16]{0:T(128)}, u32[]{:S(2)}) copy-start(s32[16]{0:T(128)} %param.13) | copy-start | bytes 196
  44.3 42.7 %all-to-all-start = ((bf16[128,16,384]{0,2,1:T(8,128)(2,1)}), bf16[128,16,384]{0,2,1:T(8,128)(2,1)}, u32[]{:S(2)}, u32[]{:S(2)}) async-start(bf16[128,16,384]{0,2,1:T(8,128)(2,1)} %bitcast.129), calls=%async_computation | async-start | bytes 3145728 | tf_op jit(solution)/shard_map/all_to_all | solution.py:52
  112.4 5.1 %copy-start.2 = (s32[128,4]{0,1:T(4,128)S(1)}, s32[128,4]{0,1:T(4,128)}, u32[]{:S(2)}) copy-start(s32[128,4]{0,1:T(4,128)} %param.14) | copy-start | bytes 6148
  112.4 43.0 %all-to-all-start.2 = ((bf16[16,128,384]{1,2,0:T(8,128)(2,1)}), bf16[16,128,384]{1,2,0:T(8,128)(2,1)}, u32[]{:S(2)}, u32[]{:S(2)}) async-start(bf16[16,128,384]{1,2,0:T(8,128)(2,1)} %bitcast.131), calls=%async_computation.2 | async-start | bytes 3145728 | tf_op jit(solution)/shard_map/all_to_all | solution.py:78
  117.5 95.5 %all-gather.2.cloned.1.call-start = ((), (), s32[]{:S(2)}) async-start(), calls=%async_computation.4 | async-start | bytes 3551232 | tf_op jit(solution)/shard_map/all_gather | solution.py:96
  158.2 59.2 %copy-start.1 = (f32[128,4]{0,1:T(4,128)S(1)}, f32[128,4]{0,1:T(4,128)}, u32[]{:S(2)}) copy-start(f32[128,4]{0,1:T(4,128)} %param.15) | copy-start | bytes 6148
  158.2 132.1 %all-reduce.8.cloned.1.call-start = ((), (), s32[]{:S(2)}) async-start(), calls=%async_computation.5 | async-start | bytes 1671168 | tf_op jit(solution)/shard_map/psum | solution.py:101
  217.4 199.3 %reduce-scatter.5.cloned.1.call-start = ((), (), s32[]{:S(2)}) async-start(), calls=%async_computation.6 | async-start | bytes 417792 | tf_op jit(solution)/shard_map/reduce_scatter | solution.py:113
  327.7 7.0 %collective-permute-start = (bf16[40,1536]{1,0:T(8,128)(2,1)S(1)}, bf16[40,1536]{1,0:T(8,128)(2,1)S(1)}, u32[]{:S(2)}, u32[]{:S(2)}) collective-permute-start(bf16[40,1536]{1,0:T(8,128)(2,1)S(1)} %fusion.2), channel_id=1, source_target_pairs={{0,64},{64,128},{128,192},{192,256},{256,320},{320,384},{384,448},... | collective-permute-start | bytes 368648
  329.0 5.7 %collective-permute-start.1 = (bf16[40,1536]{1,0:T(8,128)(2,1)S(1)}, bf16[40,1536]{1,0:T(8,128)(2,1)S(1)}, u32[]{:S(2)}, u32[]{:S(2)}) collective-permute-start(bf16[40,1536]{1,0:T(8,128)(2,1)S(1)} %fusion.2), channel_id=1, source_target_pairs={{0,128},{64,192},{128,256},{192,320},{256,384},{320,448},{384,512}... | collective-permute-start | bytes 368648
  330.3 4.3 %collective-permute-start.2 = (bf16[10,1536]{1,0:T(8,128)(2,1)S(1)}, bf16[10,1536]{1,0:T(8,128)(2,1)S(1)}, u32[]{:S(2)}, u32[]{:S(2)}) collective-permute-start(bf16[10,1536]{1,0:T(8,128)(2,1)S(1)} %slice.78), channel_id=1, source_target_pairs={{0,192},{64,256},{128,320},{192,384},{256,448},{320,512},{384,576}... | collective-permute-start | bytes 92168
Sparse Core Ops, SparseCore 0:
  158.3 54.6 all-gather.1
  217.5 72.7 all-reduce.7
  337.4 79.2 reduce-scatter.4
where the time goes:
time: 424 us; the launch traced here: 423 us
  waiting for transfers between devices  301 us (71%)
  blocking collectives  32.6 us (8%)
  matrix products  29.6 us (7%)
  starting transfers between devices  22.6 us (5%)
  local copies, waits for them, and re-layouts  15.1 us (4%)
  between operations  14.1 us (3%)
  other arithmetic  7.94 us (2%)
    reduce_scatter x1, waiting for transfers between devices, per_device(): lax.psum_scatter(term.astype(jnp.bfloat16), 'exp', scatter_dimension=0, t...  79.4 us
    psum x1, waiting for transfers between devices, per_device(): both = lax.psum(both_part.astype(jnp.bfloat16), 'rep').astype(jnp.float32)  72.3 us
    all_gather x1, waiting for transfers between devices, per_device(): lax.all_gather(picked, 'seq', axis=1, tiled=True)  54.7 us
    all_to_all x1, waiting for transfers between devices, per_device(): lax.all_to_all(result, 'seq', split_axis=0, concat_axis=1, tiled=True)  35.4 us
    all_to_all x1, waiting for transfers between devices, per_device(): lax.all_to_all(q_send, 'seq', split_axis=1, concat_axis=0, tiled=True)  35.2 us
    unnamed x1, blocking collectives  32.6 us
    all_to_all x1, waiting for transfers between devices, per_device(): lax.all_to_all(kv_send, 'seq', split_axis=1, concat_axis=0, tiled=True)  24.1 us
    sub x3, matrix products, softmax_rows(): weights = jnp.exp(scores - top)  12.9 us
  transfers between devices with their start and end apart: 9, of which 6 were waited for; matrix products, arithmetic and copies ran while one was open for 2% of the time, Pallas kernels for 0%

commit v1 on v0

v1 whole, which is shorter than its diff:
```python
import functools

import jax
import jax.numpy as jnp
from jax import lax
from jax.experimental import pallas as pl
from jax.experimental.pallas import tpu as pltpu
from jax.sharding import PartitionSpec as P

HEADS = 48
KV = 8
HD = 128
REACH = 2
CAP = 34
MAIN = 32
LEFT = CAP - MAIN
SLOTS = 48
BF = jnp.bfloat16
F32 = jnp.float32
NT = (((1,), (1,)), ((), ()))


def dot(a, b):
    return jnp.dot(a, b, preferred_element_type=F32)


def iota(shape, dim):
    return lax.broadcasted_iota(jnp.int32, shape, dim)


def attend_kernel(heads, kv_heads, q_ref, far_ref, near_ref, own_ref, low_ref, high_ref, out_ref):
    group = heads // kv_heads
    rows = group * SLOTS
    left_rows = out_ref.shape[1] - heads * MAIN
    keys_in = (REACH + 1) * own_ref.shape[0]
    key_at = iota((rows, keys_in), 1)
    allowed = (key_at >= low_ref[...]) & (key_at <= high_ref[...])
    left = jnp.zeros((left_rows, HD), F32)
    for g in range(kv_heads):
        k_cols = slice(g * HD, (g + 1) * HD)
        v_cols = slice((kv_heads + g) * HD, (kv_heads + g + 1) * HD)
        k = jnp.concatenate([ref[:, k_cols] for ref in (far_ref, near_ref, own_ref)], 0)
        v = jnp.concatenate([ref[:, v_cols] for ref in (far_ref, near_ref, own_ref)], 0)
        q = jnp.concatenate([q_ref[:, (g * group + j) * HD : (g * group + j + 1) * HD] for j in range(group)], 0)
        scores = lax.dot_general(q, k, NT, preferred_element_type=F32) * HD ** (-0.5)
        scores = jnp.where(allowed, scores, -jnp.inf)
        weights = jnp.exp(scores - jnp.max(scores, axis=1, keepdims=True))
        probs = (weights / jnp.sum(weights, axis=1, keepdims=True)).astype(BF)
        mixed = dot(probs, v).astype(BF)
        for j in range(group):
            head = g * group + j
            part = mixed[j * SLOTS : j * SLOTS + MAIN]
            for y in range(out_ref.shape[0]):
                out_ref[y, head * MAIN : (head + 1) * MAIN, :] = part
        at = iota((left_rows, rows), 0) - g * group * LEFT
        col = iota((left_rows, rows), 1)
        wanted = (at >> 1) * SLOTS + MAIN + (at & 1)
        pick = ((col == wanted) & (at >= 0) & (at < group * LEFT)).astype(F32).astype(BF)
        left = left + dot(pick, mixed)
    left = left.astype(BF)
    for y in range(out_ref.shape[0]):
        out_ref[y, heads * MAIN :, :] = left


def left_index(shape, heads, blocks, left_rows, row_dim):
    row, col = iota(shape, row_dim), iota(shape, 1 - row_dim)
    per = blocks * LEFT
    head = row // per
    inside = row - head * per
    return (col == (inside >> 1) * left_rows + head * LEFT + (inside & 1)).astype(F32).astype(BF)


def gate_kernel(heads, own_ref, sib_ref, w_ref, out_ref, x_ref):
    blocks, flat, _ = own_ref.shape
    left_rows = flat - heads * MAIN
    main, extra = blocks * MAIN, blocks * LEFT
    halves = out_ref.shape[0] // 2
    pick = left_index((heads * extra, blocks * left_rows), heads, blocks, left_rows, 0)
    for half, ref in enumerate((own_ref, sib_ref)):
        for h in range(heads):
            x_ref[:main, h * HD : (h + 1) * HD] = ref[:, h * MAIN : (h + 1) * MAIN, :].reshape(main, HD)
        left = dot(pick, ref[:, heads * MAIN :, :].reshape(blocks * left_rows, HD)).astype(BF)
        for h in range(heads):
            x_ref[main:, h * HD : (h + 1) * HD] = left[h * extra : (h + 1) * extra]
        x = x_ref[...]
        for part in range(2):
            both = lax.dot_general(x, w_ref[0, part], NT, preferred_element_type=F32)
            m, n = main // halves, extra // halves
            for j in range(halves):
                rows = jnp.concatenate([both[j * m : (j + 1) * m], both[main + j * n : main + (j + 1) * n]], 0)
                out_ref[half * halves + j, part] = rows.astype(BF)


def hidden_kernel(in_ref, out_ref):
    n = in_ref.shape[0]
    gate = sum(in_ref[i, 0].astype(F32) for i in range(n))
    up = sum(in_ref[i, 1].astype(F32) for i in range(n))
    hidden = (gate / (1.0 + jnp.exp(-gate)) * up).astype(BF)
    for i in range(n):
        out_ref[i] = hidden


def down_kernel(heads, hid_ref, w_ref, own_ref, sib_ref):
    blocks, flat, _ = own_ref.shape
    left_rows = flat - heads * MAIN
    main, extra = blocks * MAIN, blocks * LEFT
    halves = hid_ref.shape[0] // 2
    m = main // halves
    put = left_index((blocks * left_rows, heads * extra), heads, blocks, left_rows, 1)
    for half, ref in enumerate((own_ref, sib_ref)):
        chunks = [hid_ref[half * halves + j].astype(F32) for j in range(halves)]
        hidden = jnp.concatenate([c[:m] for c in chunks] + [c[m:] for c in chunks], 0).astype(BF)
        out = dot(hidden, w_ref[0]).astype(BF)
        for h in range(heads):
            ref[:, h * MAIN : (h + 1) * MAIN, :] = out[:main, h * HD : (h + 1) * HD].reshape(blocks, MAIN, HD)
        stack = jnp.concatenate([out[main:, h * HD : (h + 1) * HD] for h in range(heads)], 0)
        ref[:, heads * MAIN :, :] = dot(put, stack).astype(BF).reshape(blocks, left_rows, HD)


def owner_kernel(heads, in_ref, put_ref, share_ref, left_share_ref, out_ref, x_ref):
    flat = in_ref.shape[1]
    left_rows = flat - heads * MAIN
    total = sum(in_ref[y].astype(F32) for y in range(in_ref.shape[0]))
    share = share_ref[...]
    left = (total[heads * MAIN :] * left_share_ref[...]).astype(BF)
    rest = SLOTS - MAIN
    row, col = iota((heads * rest, left_rows), 0), iota((heads * rest, left_rows), 1)
    head = row // rest
    inside = row - head * rest
    pick = ((col == head * LEFT + inside) & (inside < LEFT)).astype(F32).astype(BF)
    left = dot(pick, left).astype(BF)
    for h in range(heads):
        cols = slice(h * HD, (h + 1) * HD)
        x_ref[:MAIN, cols] = (total[h * MAIN : (h + 1) * MAIN] * share).astype(BF)
        x_ref[MAIN:, cols] = left[h * rest : (h + 1) * rest]
    out_ref[...] = dot(put_ref[...], x_ref[...]).astype(BF)


def call(kernel, shapes, scratch=(), flops=0, moved=0):
    return pl.pallas_call(
        kernel,
        out_shape=shapes,
        scratch_shapes=list(scratch),
        compiler_params=pltpu.CompilerParams(vmem_limit_bytes=48 * 1024 * 1024),
        cost_estimate=pl.CostEstimate(flops=flops, bytes_accessed=moved, transcendentals=0),
    )


def per_device(queries, keys, values, lengths, expert_ids, gate_share, gate_up, down_t):
    n_seq, n_exp, n_rep = (lax.axis_size(a) for a in ("seq", "exp", "rep"))
    tok = queries.shape[0]
    cols = gate_up.shape[1]
    hid = gate_up.shape[3]
    heads, kv_heads = cols // HD, KV // n_rep
    group = heads // kv_heads
    n_y = n_seq // 2
    left_rows = -(-heads * LEFT // 16) * 16
    flat = heads * MAIN + left_rows
    seq_at, exp_at, rep_at = (lax.axis_index(a) for a in ("seq", "exp", "rep"))
    same_core = [[2 * y + c for y in range(n_y)] for c in range(2)]
    sibling = [(i, i ^ 1) for i in range(n_seq)]

    kv_cols = kv_heads * HD
    kv = jnp.concatenate(
        [
            lax.dynamic_slice_in_dim(keys, rep_at * kv_cols, kv_cols, 1),
            lax.dynamic_slice_in_dim(values, rep_at * kv_cols, kv_cols, 1),
        ],
        1,
    )
    far = lax.ppermute(kv, "seq", [(i, (i + 2) % n_seq) for i in range(n_seq)])
    near = lax.ppermute(kv, "seq", [(i, (i + 1) % n_seq) for i in range(n_seq)])

    hit = expert_ids == exp_at
    match = jnp.any(hit, axis=1).astype(jnp.int32)
    share_of = jnp.sum(jnp.where(hit, gate_share, 0.0), axis=1)
    rank = jnp.cumsum(match) - match
    slot = jnp.where(match > 0, rank, -1)
    pick = slot[None, :] == jnp.arange(SLOTS, dtype=jnp.int32)[:, None]
    put = (slot[:, None] == jnp.arange(SLOTS, dtype=jnp.int32)[None, :]).astype(BF)
    place = jnp.arange(tok, dtype=jnp.int32)
    ends = jnp.cumsum(lengths)
    starts = jnp.max(jnp.where(ends[None, :] <= seq_at * tok + place[:, None], ends[None, :], 0), axis=1)
    low_of = starts - (seq_at - REACH) * tok
    low = jnp.sum(jnp.where(pick, low_of[None, :], 0), axis=1)
    high = jnp.sum(jnp.where(pick, place[None, :], 0), axis=1) + REACH * tok
    share = jnp.sum(jnp.where(pick, share_of[None, :], 0.0), axis=1)
    left_share = jnp.tile(share[MAIN:CAP], left_rows // LEFT)
    q_cols = lax.dynamic_slice_in_dim(queries, rep_at * cols, cols, 1)
    q_rows = dot(pick.astype(BF), q_cols).astype(BF)

    spread = call(
        functools.partial(attend_kernel, heads, kv_heads),
        jax.ShapeDtypeStruct((n_y, flat, HD), BF),
        flops=4 * heads * SLOTS * 3 * tok * HD,
    )(q_rows, far, near, kv, jnp.tile(low, group)[:, None], jnp.tile(high, group)[:, None])

    own = lax.all_to_all(spread, "seq", split_axis=0, concat_axis=0, tiled=True, axis_index_groups=same_core)
    sib = lax.ppermute(own, "seq", sibling)

    rows = n_seq * CAP // n_rep
    gate_w = jnp.transpose(gate_up, (0, 2, 3, 1))
    down_w = jnp.transpose(down_t, (0, 2, 1))
    parts = call(
        functools.partial(gate_kernel, heads),
        jax.ShapeDtypeStruct((n_rep, 2, rows, hid), BF),
        [pltpu.VMEM((n_y * CAP, cols), BF)],
        flops=4 * n_seq * CAP * cols * hid,
    )(own, sib, gate_w)
    parts = lax.all_to_all(parts, "rep", split_axis=0, concat_axis=0, tiled=True)
    hidden = call(hidden_kernel, jax.ShapeDtypeStruct((n_rep, rows, hid), BF))(parts)
    hidden = lax.all_to_all(hidden, "rep", split_axis=0, concat_axis=0, tiled=True)
    mine, theirs = call(
        functools.partial(down_kernel, heads),
        [jax.ShapeDtypeStruct((n_y, flat, HD), BF)] * 2,
        flops=2 * n_seq * CAP * cols * hid,
    )(hidden, down_w)
    back = lax.ppermute(theirs, "seq", sibling)
    mine = (mine.astype(F32) + back.astype(F32)).astype(BF)
    mine = lax.all_to_all(mine, "seq", split_axis=0, concat_axis=0, tiled=True, axis_index_groups=same_core)
    term = call(
        functools.partial(owner_kernel, heads),
        jax.ShapeDtypeStruct((tok, cols), BF),
        [pltpu.VMEM((SLOTS, cols), BF)],
        flops=2 * SLOTS * tok * cols,
    )(mine, put, share[:MAIN, None], left_share[:, None])
    terms = lax.all_to_all(term.reshape(n_exp, tok // n_exp, cols), "exp", split_axis=0, concat_axis=0, tiled=True)
    return jnp.sum(terms.astype(F32), axis=0).astype(BF)


def solution(mesh):
    in_specs = (
        P("seq", None),
        P("seq", None),
        P("seq", None),
        P(),
        P("seq", None),
        P("seq", None),
        P("exp", "rep", None, "seq"),
        P("exp", "rep", "seq"),
    )
    return jax.shard_map(
        per_device, mesh=mesh, in_specs=in_specs, out_specs=P(("seq", "exp"), "rep"), check_vma=False
    )
```

time: 424 us -> 159 us (0.38)
  waiting for transfers between devices: 301 us -> 33.9 us
  blocking collectives: 32.6 us -> 101 us
  matrix products: 29.6 us -> 0.2 us
  between operations: 14.1 us -> 0.2 us
  local copies, waits for them, and re-layouts: 15.1 us -> 2.35 us
  starting transfers between devices: 22.6 us -> 11 us
  Pallas kernels: 0 us -> 5.34 us
  other arithmetic: 7.94 us -> 3.4 us
    all_to_all x0 -> x4, blocking collectives: none -> 101 us  [the longest x1 28.3 us: per_device(): lax.all_to_all(spread, 'seq', split_axis=0, concat_axis=0, tiled=True, ax...]
    reduce_scatter x1 -> x0, waiting for transfers between devices: 79.4 us -> none  [per_device(): lax.psum_scatter(term.astype(jnp.bfloat16), 'exp', scatter_dimension=0, t...]
    psum x1 -> x0, waiting for transfers between devices: 72.3 us -> none  [per_device(): both = lax.psum(both_part.astype(jnp.bfloat16), 'rep').astype(jnp.float32)]
    all_to_all x3 -> x1, waiting for transfers between devices: 94.7 us -> 24.6 us  [per_device(): lax.all_to_all(mine, 'seq', split_axis=0, concat_axis=0, tiled=True, axis...]
    all_gather x1 -> x0, waiting for transfers between devices: 54.7 us -> none  [per_device(): lax.all_gather(picked, 'seq', axis=1, tiled=True)]
    unnamed x1 -> x0, blocking collectives: 32.6 us -> none
    dot_general x5 -> x1, matrix products: 16.8 us -> 0.2 us  [dot(): return jnp.dot(a, b, preferred_element_type=F32)]
    all_to_all x3 -> x1, starting transfers between devices: 17.5 us -> 3.55 us  [per_device(): lax.all_to_all(mine, 'seq', split_axis=0, concat_axis=0, tiled=True, axis...]
  transfers between devices with their start and end apart: 9 -> 5, of which waited for: 6 -> 5; matrix products, arithmetic and copies ran while one was open for 2% -> 2% of each run, Pallas kernels for 0% -> 0%
where the time goes in v1:
time: 159 us; the launch traced here: 157 us
  blocking collectives  101 us (64%)
  waiting for transfers between devices  33.9 us (21%)
  starting transfers between devices  11 us (7%)
  Pallas kernels  5.34 us (3%)
  other arithmetic  3.4 us (2%)
  local copies, waits for them, and re-layouts  2.35 us (1%)
    all_to_all x1, blocking collectives, per_device(): lax.all_to_all(spread, 'seq', split_axis=0, concat_axis=0, tiled=True, ax...  28.3 us
    all_to_all x1, blocking collectives, per_device(): lax.all_to_all(term.reshape(n_exp, tok // n_exp, cols), 'exp', split_axis...  27.1 us
    all_to_all x1, blocking collectives, per_device(): lax.all_to_all(parts, 'rep', split_axis=0, concat_axis=0, tiled=True)  25.2 us
    all_to_all x1, waiting for transfers between devices, per_device(): lax.all_to_all(mine, 'seq', split_axis=0, concat_axis=0, tiled=True, axis...  24.6 us
    all_to_all x1, blocking collectives, per_device(): lax.all_to_all(hidden, 'rep', split_axis=0, concat_axis=0, tiled=True)  20.5 us
    ppermute x1, waiting for transfers between devices, per_device(): far = lax.ppermute(kv, 'seq', [(i, (i + 2) % n_seq) for i in range(n_seq)])  4.08 us
    ppermute x1, starting transfers between devices, per_device(): far = lax.ppermute(kv, 'seq', [(i, (i + 2) % n_seq) for i in range(n_seq)])  3.6 us
    all_to_all x1, starting transfers between devices, per_device(): lax.all_to_all(mine, 'seq', split_axis=0, concat_axis=0, tiled=True, axis...  3.55 us
  transfers between devices with their start and end apart: 5, of which 5 were waited for; matrix products, arithmetic and copies ran while one was open for 2% of the time, Pallas kernels for 0%

profile of v1, /device:TPU:14, one launch (start us, length us, event | category | flops | bytes accessed | tf_op | source)
XLA Modules:
  0.0 157.5 jit_solution(2994611541046675193)
XLA Ops:
  0.0 1.0 constant_dynamic-slice_fusion
  1.0 3.6 %collective-permute-start = (bf16[128,512]{1,0:T(8,128)(2,1)S(1)}, bf16[128,512]{1,0:T(8,128)(2,1)S(1)}, u32[]{:S(2)}, u32[]{:S(2)}) collective-permute-start(bf16[128,512]{1,0:T(8,128)(2,1)S(1)} %pad_maximum_fusion.own_ref), channel_id=1, source_target_pairs={{0,128},{64,192},{128,256},{192,320},{256,384},{320,448},{384,512}... | collective-permute-start | bytes 393224 | tf_op jit(solution)/shard_map/ppermute | solution.py:171
  4.7 0.7 select_reduce_fusion.4
  5.5 0.2 reduce-window.15
  5.8 0.7 copy.20
  7.2 0.2 convolution_convert_fusion.q_ref
  7.4 4.1 %collective-permute-done.far_ref = bf16[128,512]{1,0:T(8,128)(2,1)S(1)} collective-permute-done((bf16[128,512]{1,0:T(8,128)(2,1)S(1)}, bf16[128,512]{1,0:T(8,128)(2,1)S(1)}, u32[]{:S(2)}, u32[]{:S(2)}) %collective-permute-start) | collective-permute-done | bytes 131104 | tf_op jit(solution)/shard_map/ppermute | solution.py:171
  11.5 0.6 collective-permute-done.1.near_ref
  12.1 1.2 shard_map.82
  13.3 28.3 %all_to_all.25.own_ref = bf16[8,416,128]{2,1,0:T(8,128)(2,1)S(1)} all-to-all(bf16[8,416,128]{2,1,0:T(8,128)(2,1)S(1)} %shard_map.82), channel_id=1, replica_groups={{0,128,256,384,512,640,768,896},{64,192,320,448,576,704,832,960},{1,129..., dimensions={0} | all-to-all | bytes 1703936 | tf_op jit(solution)/shard_map/all_to_all | solution.py:198
  41.6 1.9 %collective-permute-start.2 = (bf16[8,416,128]{2,1,0:T(8,128)(2,1)S(1)}, bf16[8,416,128]{2,1,0:T(8,128)(2,1)S(1)}, u32[]{:S(2)}, u32[]{:S(2)}) collective-permute-start(bf16[8,416,128]{2,1,0:T(8,128)(2,1)S(1)} %all_to_all.25.own_ref), channel_id=1, source_target_pairs={{0,64},{64,0},{128,192},{192,128},{256,320},{320,256},{384,448},{4... | collective-permute-start | bytes 2555912 | tf_op jit(solution)/shard_map/ppermute | solution.py:199
  43.5 2.3 %collective-permute-done.2.sib_ref = bf16[8,416,128]{2,1,0:T(8,128)(2,1)S(1)} collective-permute-done((bf16[8,416,128]{2,1,0:T(8,128)(2,1)S(1)}, bf16[8,416,128]{2,1,0:T(8,128)(2,1)S(1)}, u32[]{:S(2)}, u32[]{:S(2)}) %collective-permute-start.2) | collective-permute-done | bytes 852000 | tf_op jit(solution)/shard_map/ppermute | solution.py:199
  45.9 2.1 %shard_map.83 = bf16[4,2,136,336]{3,2,1,0:T(8,128)(2,1)S(1)} custom-call(bf16[8,416,128]{2,1,0:T(8,128)(2,1)S(1)} %all_to_all.25.own_ref, bf16[8,416,128]{2,1,0:T(8,128)(2,1)S(1)} %collective-permute-done.2.sib_ref, bf16[1,2,336,1536]{3,2,1,0:T(8,128)(2,1)S(1)} %bitcast.8), custom_call_target="tpu_custom_call" | custom-call | flops 1123024896 | tf_op jit(solution)/shard_map/pallas_call | solution.py:204
  48.0 25.2 %all_to_all.26.in_ref = bf16[4,2,136,336]{3,2,1,0:T(8,128)(2,1)S(1)} all-to-all(bf16[4,2,136,336]{3,2,1,0:T(8,128)(2,1)S(1)} %shard_map.83), channel_id=1, replica_groups=mesh['seq'=16,'exp'=16,'rep'=4] {'rep'}, dimensions={0} | all-to-all | bytes 1462272 | tf_op jit(solution)/shard_map/all_to_all | solution.py:210
  73.3 20.5 %all_to_all.27.hid_ref = bf16[4,136,336]{2,1,0:T(8,128)(2,1)S(1)} all-to-all(bf16[4,136,336]{2,1,0:T(8,128)(2,1)S(1)} %shard_map.84), channel_id=1, replica_groups=mesh['seq'=16,'exp'=16,'rep'=4] {'rep'}, dimensions={0} | all-to-all | bytes 731136 | tf_op jit(solution)/shard_map/all_to_all | solution.py:212
  93.9 1.4 shard_map.85
  95.3 1.9 %collective-permute-start.3 = (bf16[8,416,128]{2,1,0:T(8,128)(2,1)S(1)}, bf16[8,416,128]{2,1,0:T(8,128)(2,1)S(1)}, u32[]{:S(2)}, u32[]{:S(2)}) collective-permute-start(bf16[8,416,128]{2,1,0:T(8,128)(2,1)S(1)} %get-tuple-element.8), channel_id=1, source_target_pairs={{0,64},{64,0},{128,192},{192,128},{256,320},{320,256},{384,448},{4... | collective-permute-start | bytes 2555912 | tf_op jit(solution)/shard_map/ppermute | solution.py:218
  97.2 2.3 %collective-permute-done.3 = bf16[8,416,128]{2,1,0:T(8,128)(2,1)S(1)} collective-permute-done((bf16[8,416,128]{2,1,0:T(8,128)(2,1)S(1)}, bf16[8,416,128]{2,1,0:T(8,128)(2,1)S(1)}, u32[]{:S(2)}, u32[]{:S(2)}) %collective-permute-start.3) | collective-permute-done | bytes 852000 | tf_op jit(solution)/shard_map/ppermute | solution.py:218
  99.6 1.1 add_convert_fusion
  100.7 3.5 %all-to-all-start.3 = ((bf16[8,416,128]{2,1,0:T(8,128)(2,1)}), bf16[8,416,128]{2,1,0:T(8,128)(2,1)S(1)}, u32[]{:S(2)}, u32[]{:S(2)}) async-start(bf16[8,416,128]{2,1,0:T(8,128)(2,1)} %add_convert_fusion), calls=%async_computation.3 | async-start | bytes 1703936 | tf_op jit(solution)/shard_map/all_to_all | solution.py:220
  104.7 24.6 %all-to-all-done.3.in_ref = bf16[8,416,128]{2,1,0:T(8,128)(2,1)S(1)} async-done(((bf16[8,416,128]{2,1,0:T(8,128)(2,1)}), bf16[8,416,128]{2,1,0:T(8,128)(2,1)S(1)}, u32[]{:S(2)}, u32[]{:S(2)}) %all-to-all-start.3) | async-done | bytes 852000 | tf_op jit(solution)/shard_map/all_to_all | solution.py:220
  129.3 0.5 shard_map.86
  129.7 27.1 %all_to_all.28 = bf16[16,8,1536]{2,1,0:T(8,128)(2,1)S(1)} all-to-all(bf16[16,8,1536]{2,1,0:T(8,128)(2,1)S(1)} %bitcast.9), channel_id=1, replica_groups=mesh['seq'=16,'exp'=16,'rep'=4] {'exp'}, dimensions={0} | all-to-all | bytes 786432 | tf_op jit(solution)/shard_map/all_to_all | solution.py:227
  156.8 0.7 reduce_sum.52
  (32 shorter events, 1.5 us)
Async XLA Ops:
  0.0 7.2 %copy-start = (bf16[128,6144]{1,0:T(8,128)(2,1)S(1)}, bf16[128,6144]{1,0:T(8,128)(2,1)}, u32[]{:S(2)}) copy-start(bf16[128,6144]{1,0:T(8,128)(2,1)} %param.8) | copy-start | bytes 4718596
  1.0 10.5 %collective-permute-start = (bf16[128,512]{1,0:T(8,128)(2,1)S(1)}, bf16[128,512]{1,0:T(8,128)(2,1)S(1)}, u32[]{:S(2)}, u32[]{:S(2)}) collective-permute-start(bf16[128,512]{1,0:T(8,128)(2,1)S(1)} %pad_maximum_fusion.own_ref), channel_id=1, source_target_pairs={{0,128},{64,192},{128,256},{192,320},{256,384},{320,448},{384,512}... | collective-permute-start | bytes 393224 | tf_op jit(solution)/shard_map/ppermute | solution.py:171
  4.6 7.5 %collective-permute-start.1 = (bf16[128,512]{1,0:T(8,128)(2,1)S(1)}, bf16[128,512]{1,0:T(8,128)(2,1)S(1)}, u32[]{:S(2)}, u32[]{:S(2)}) collective-permute-start(bf16[128,512]{1,0:T(8,128)(2,1)S(1)} %pad_maximum_fusion.own_ref), channel_id=1, source_target_pairs={{0,64},{64,128},{128,192},{192,256},{256,320},{320,384},{384,448},... | collective-permute-start | bytes 393224 | tf_op jit(solution)/shard_map/ppermute | solution.py:172
  7.4 38.4 %copy-start.1 = (bf16[1,1536,2,336]{1,3,2,0:T(8,128)(2,1)S(1)}, bf16[1,1536,2,336]{1,3,2,0:T(8,128)(2,1)}, u32[]{:S(2)}) copy-start(bf16[1,1536,2,336]{1,3,2,0:T(8,128)(2,1)} %param.14) | copy-start | bytes 6193156
  41.6 4.3 %collective-permute-start.2 = (bf16[8,416,128]{2,1,0:T(8,128)(2,1)S(1)}, bf16[8,416,128]{2,1,0:T(8,128)(2,1)S(1)}, u32[]{:S(2)}, u32[]{:S(2)}) collective-permute-start(bf16[8,416,128]{2,1,0:T(8,128)(2,1)S(1)} %all_to_all.25.own_ref), channel_id=1, source_target_pairs={{0,64},{64,0},{128,192},{192,128},{256,320},{320,256},{384,448},{4... | collective-permute-start | bytes 2555912 | tf_op jit(solution)/shard_map/ppermute | solution.py:199
  48.0 45.9 %copy-start.2 = (bf16[1,1536,336]{1,2,0:T(8,128)(2,1)S(1)}, bf16[1,1536,336]{1,2,0:T(8,128)(2,1)}, u32[]{:S(2)}) copy-start(bf16[1,1536,336]{1,2,0:T(8,128)(2,1)} %param.15) | copy-start | bytes 3096580
  95.3 4.3 %collective-permute-start.3 = (bf16[8,416,128]{2,1,0:T(8,128)(2,1)S(1)}, bf16[8,416,128]{2,1,0:T(8,128)(2,1)S(1)}, u32[]{:S(2)}, u32[]{:S(2)}) collective-permute-start(bf16[8,416,128]{2,1,0:T(8,128)(2,1)S(1)} %get-tuple-element.8), channel_id=1, source_target_pairs={{0,64},{64,0},{128,192},{192,128},{256,320},{320,256},{384,448},{4... | collective-permute-start | bytes 2555912 | tf_op jit(solution)/shard_map/ppermute | solution.py:218
  100.7 28.6 %all-to-all-start.3 = ((bf16[8,416,128]{2,1,0:T(8,128)(2,1)}), bf16[8,416,128]{2,1,0:T(8,128)(2,1)S(1)}, u32[]{:S(2)}, u32[]{:S(2)}) async-start(bf16[8,416,128]{2,1,0:T(8,128)(2,1)} %add_convert_fusion), calls=%async_computation.3 | async-start | bytes 1703936 | tf_op jit(solution)/shard_map/all_to_all | solution.py:220

commit v2 on v1

--- a/solution.py
+++ b/solution.py
@@ -70,25 +70,35 @@
     return (col == (inside >> 1) * left_rows + head * LEFT + (inside & 1)).astype(F32).astype(BF)
 
 
-def gate_kernel(heads, own_ref, sib_ref, w_ref, out_ref, x_ref):
-    blocks, flat, _ = own_ref.shape
+def own_of(shape, row_dim, n, per):
+    row, col = iota(shape, row_dim), iota(shape, 1 - row_dim)
+    chunk = row // (2 * per)
+    inside = row - chunk * 2 * per
+    shard = inside // per
+    return (col == shard * n * per + chunk * per + inside - shard * per).astype(F32).astype(BF)
+
+
+def gate_kernel(heads, in_ref, own_w_ref, sib_w_ref, out_ref, x_ref):
+    blocks, flat, _ = in_ref.shape
+    chunks = out_ref.shape[0]
     left_rows = flat - heads * MAIN
     main, extra = blocks * MAIN, blocks * LEFT
-    halves = out_ref.shape[0] // 2
+    m, n = main // chunks, extra // chunks
     pick = left_index((heads * extra, blocks * left_rows), heads, blocks, left_rows, 0)
-    for half, ref in enumerate((own_ref, sib_ref)):
-        for h in range(heads):
-            x_ref[:main, h * HD : (h + 1) * HD] = ref[:, h * MAIN : (h + 1) * MAIN, :].reshape(main, HD)
-        left = dot(pick, ref[:, heads * MAIN :, :].reshape(blocks * left_rows, HD)).astype(BF)
-        for h in range(heads):
-            x_ref[main:, h * HD : (h + 1) * HD] = left[h * extra : (h + 1) * extra]
-        x = x_ref[...]
-        for part in range(2):
-            both = lax.dot_general(x, w_ref[0, part], NT, preferred_element_type=F32)
-            m, n = main // halves, extra // halves
-            for j in range(halves):
-                rows = jnp.concatenate([both[j * m : (j + 1) * m], both[main + j * n : main + (j + 1) * n]], 0)
-                out_ref[half * halves + j, part] = rows.astype(BF)
+    for h in range(heads):
+        x_ref[:main, h * HD : (h + 1) * HD] = in_ref[:, h * MAIN : (h + 1) * MAIN, :].reshape(main, HD)
+    left = dot(pick, in_ref[:, heads * MAIN :, :].reshape(blocks * left_rows, HD)).astype(BF)
+    for h in range(heads):
+        x_ref[main:, h * HD : (h + 1) * HD] = left[h * extra : (h + 1) * extra]
+    x = x_ref[...]
+    order = own_of((2 * extra, 2 * extra), 0, chunks, n)
+    for part in range(2):
+        own = lax.dot_general(x, own_w_ref[0, part], NT, preferred_element_type=F32)
+        sib = lax.dot_general(x, sib_w_ref[0, part], NT, preferred_element_type=F32)
+        left = dot(order, jnp.concatenate([own[main:], sib[main:]], 0).astype(BF))
+        for j in range(chunks):
+            rows = [own[j * m : (j + 1) * m], sib[j * m : (j + 1) * m], left[j * 2 * n : (j + 1) * 2 * n]]
+            out_ref[j, part] = jnp.concatenate(rows, 0).astype(BF)
 
 
 def hidden_kernel(in_ref, out_ref):
@@ -100,21 +110,23 @@
         out_ref[i] = hidden
 
 
-def down_kernel(heads, hid_ref, w_ref, own_ref, sib_ref):
-    blocks, flat, _ = own_ref.shape
+def down_kernel(heads, hid_ref, own_w_ref, sib_w_ref, out_ref):
+    blocks, flat, _ = out_ref.shape
+    chunks = hid_ref.shape[0]
     left_rows = flat - heads * MAIN
     main, extra = blocks * MAIN, blocks * LEFT
-    halves = hid_ref.shape[0] // 2
-    m = main // halves
+    m, n = main // chunks, extra // chunks
     put = left_index((blocks * left_rows, heads * extra), heads, blocks, left_rows, 1)
-    for half, ref in enumerate((own_ref, sib_ref)):
-        chunks = [hid_ref[half * halves + j].astype(F32) for j in range(halves)]
-        hidden = jnp.concatenate([c[:m] for c in chunks] + [c[m:] for c in chunks], 0).astype(BF)
-        out = dot(hidden, w_ref[0]).astype(BF)
-        for h in range(heads):
-            ref[:, h * MAIN : (h + 1) * MAIN, :] = out[:main, h * HD : (h + 1) * HD].reshape(blocks, MAIN, HD)
-        stack = jnp.concatenate([out[main:, h * HD : (h + 1) * HD] for h in range(heads)], 0)
-        ref[:, heads * MAIN :, :] = dot(put, stack).astype(BF).reshape(blocks, left_rows, HD)
+    held = [hid_ref[j].astype(F32) for j in range(chunks)]
+    order = own_of((2 * extra, 2 * extra), 1, chunks, n)
+    left = dot(order, jnp.concatenate([c[2 * m :] for c in held], 0).astype(BF))
+    own = jnp.concatenate([c[:m] for c in held] + [left[:extra]], 0).astype(BF)
+    sib = jnp.concatenate([c[m : 2 * m] for c in held] + [left[extra:]], 0).astype(BF)
+    out = (dot(own, own_w_ref[0]) + dot(sib, sib_w_ref[0])).astype(BF)
+    for h in range(heads):
+        out_ref[:, h * MAIN : (h + 1) * MAIN, :] = out[:main, h * HD : (h + 1) * HD].reshape(blocks, MAIN, HD)
+    stack = jnp.concatenate([out[main:, h * HD : (h + 1) * HD] for h in range(heads)], 0)
+    out_ref[:, heads * MAIN :, :] = dot(put, stack).astype(BF).reshape(blocks, left_rows, HD)
 
 
 def owner_kernel(heads, in_ref, put_ref, share_ref, left_share_ref, out_ref, x_ref):
@@ -195,28 +207,27 @@
         flops=4 * heads * SLOTS * 3 * tok * HD,
     )(q_rows, far, near, kv, jnp.tile(low, group)[:, None], jnp.tile(high, group)[:, None])
 
-    own = lax.all_to_all(spread, "seq", split_axis=0, concat_axis=0, tiled=True, axis_index_groups=same_core)
-    sib = lax.ppermute(own, "seq", sibling)
-
-    rows = n_seq * CAP // n_rep
     gate_w = jnp.transpose(gate_up, (0, 2, 3, 1))
     down_w = jnp.transpose(down_t, (0, 2, 1))
+    sib_gate_w = lax.ppermute(gate_w, "seq", sibling)
+    sib_down_w = lax.ppermute(down_w, "seq", sibling)
+    mine = lax.all_to_all(spread, "seq", split_axis=0, concat_axis=0, tiled=True, axis_index_groups=same_core)
+
+    rows = 2 * n_y * CAP // n_rep
     parts = call(
         functools.partial(gate_kernel, heads),
         jax.ShapeDtypeStruct((n_rep, 2, rows, hid), BF),
         [pltpu.VMEM((n_y * CAP, cols), BF)],
-        flops=4 * n_seq * CAP * cols * hid,
-    )(own, sib, gate_w)
+        flops=8 * n_y * CAP * cols * hid,
+    )(mine, gate_w, sib_gate_w)
     parts = lax.all_to_all(parts, "rep", split_axis=0, concat_axis=0, tiled=True)
     hidden = call(hidden_kernel, jax.ShapeDtypeStruct((n_rep, rows, hid), BF))(parts)
     hidden = lax.all_to_all(hidden, "rep", split_axis=0, concat_axis=0, tiled=True)
-    mine, theirs = call(
+    mine = call(
         functools.partial(down_kernel, heads),
-        [jax.ShapeDtypeStruct((n_y, flat, HD), BF)] * 2,
-        flops=2 * n_seq * CAP * cols * hid,
-    )(hidden, down_w)
-    back = lax.ppermute(theirs, "seq", sibling)
-    mine = (mine.astype(F32) + back.astype(F32)).astype(BF)
+        jax.ShapeDtypeStruct((n_y, flat, HD), BF),
+        flops=4 * n_y * CAP * cols * hid,
+    )(hidden, down_w, sib_down_w)
     mine = lax.all_to_all(mine, "seq", split_axis=0, concat_axis=0, tiled=True, axis_index_groups=same_core)
     term = call(
         functools.partial(owner_kernel, heads),

time: 159 us -> 150 us (0.943)
  blocking collectives: 101 us -> 67.8 us
  starting transfers between devices: 11 us -> 33.1 us
  Pallas kernels: 5.34 us -> 10.8 us
    all_to_all x2 -> x0, blocking collectives: 45.7 us -> none  [the longest x1 25.2 us: per_device(): lax.all_to_all(parts, 'rep', split_axis=0, concat_axis=0, tiled=True)]
    all_to_all x0 -> x2, starting transfers between devices: none -> 18.9 us  [the longest x1 11.7 us: per_device(): lax.all_to_all(hidden, 'rep', split_axis=0, concat_axis=0, tiled=True)]
    all_to_all x0 -> x2, waiting for transfers between devices: none -> 15.4 us  [the longest x1 9.01 us: per_device(): lax.all_to_all(parts, 'rep', split_axis=0, concat_axis=0, tiled=True)]
    all_to_all x1, blocking collectives: 27.1 us -> 38.5 us  [per_device(): lax.all_to_all(term.reshape(n_exp, tok // n_exp, cols), 'exp', split_axis...]
    all_to_all x1, waiting for transfers between devices: 24.6 us -> 16.4 us  [per_device(): lax.all_to_all(mine, 'seq', split_axis=0, concat_axis=0, tiled=True, axis...]
    ppermute x2, waiting for transfers between devices: 4.69 us -> 0.01 us  [the longest x1 0.01 us: per_device(): sib_gate_w = lax.ppermute(gate_w, 'seq', sibling)]
    ppermute x1, waiting for transfers between devices: 4.08 us -> 0.37 us  [per_device(): far = lax.ppermute(kv, 'seq', [(i, (i + 2) % n_seq) for i in range(n_seq)])]
    pallas_call x1, Pallas kernels: 2.1 us -> 4.69 us  [per_device(): call(functools.partial(gate_kernel, heads), jax.ShapeDtypeStruct((n_rep,...]
  transfers between devices with their start and end apart: 5 -> 7, of which waited for: 5 -> 5; matrix products, arithmetic and copies ran while one was open for 2% -> 2% of each run, Pallas kernels for 0% -> 1%
where the time goes in v2:
time: 150 us
  blocking collectives  67.8 us (45%)
  starting transfers between devices  33.1 us (22%)
  waiting for transfers between devices  32.8 us (22%)
  Pallas kernels  10.8 us (7%)
  local copies, waits for them, and re-layouts  2.35 us (2%)
  other arithmetic  2.27 us (2%)
    all_to_all x1, blocking collectives, per_device(): lax.all_to_all(term.reshape(n_exp, tok // n_exp, cols), 'exp', split_axis...  38.5 us
    all_to_all x1, blocking collectives, per_device(): lax.all_to_all(spread, 'seq', split_axis=0, concat_axis=0, tiled=True, ax...  29.3 us
    all_to_all x1, waiting for transfers between devices, per_device(): lax.all_to_all(mine, 'seq', split_axis=0, concat_axis=0, tiled=True, axis...  16.4 us
    all_to_all x1, starting transfers between devices, per_device(): lax.all_to_all(hidden, 'rep', split_axis=0, concat_axis=0, tiled=True)  11.7 us
    all_to_all x1, waiting for transfers between devices, per_device(): lax.all_to_all(parts, 'rep', split_axis=0, concat_axis=0, tiled=True)  9.01 us
    all_to_all x1, starting transfers between devices, per_device(): lax.all_to_all(parts, 'rep', split_axis=0, concat_axis=0, tiled=True)  7.28 us
    all_to_all x1, waiting for transfers between devices, per_device(): lax.all_to_all(hidden, 'rep', split_axis=0, concat_axis=0, tiled=True)  6.44 us
    all_to_all x1, starting transfers between devices, per_device(): lax.all_to_all(mine, 'seq', split_axis=0, concat_axis=0, tiled=True, axis...  4.93 us
  transfers between devices with their start and end apart: 7, of which 5 were waited for; matrix products, arithmetic and copies ran while one was open for 2% of the time, Pallas kernels for 1%

profile of v2, /device:TPU:14, one launch (start us, length us, event | category | flops | bytes accessed | tf_op | source)
XLA Modules:
  0.0 149.5 jit_solution(17348115373176796763)
XLA Ops:
  0.0 1.0 constant_dynamic-slice_fusion
  1.0 3.6 %collective-permute-start = (bf16[128,512]{1,0:T(8,128)(2,1)S(1)}, bf16[128,512]{1,0:T(8,128)(2,1)S(1)}, u32[]{:S(2)}, u32[]{:S(2)}) collective-permute-start(bf16[128,512]{1,0:T(8,128)(2,1)S(1)} %pad_maximum_fusion.own_ref), channel_id=1, source_target_pairs={{0,128},{64,192},{128,256},{192,320},{256,384},{320,448},{384,512}... | collective-permute-start | bytes 393224 | tf_op jit(solution)/shard_map/ppermute | solution.py:183
  4.7 3.7 %collective-permute-start.2 = (bf16[1,2,336,1536]{3,2,1,0:T(8,128)(2,1)}, bf16[1,2,336,1536]{3,2,1,0:T(8,128)(2,1)}, u32[]{:S(2)}, u32[]{:S(2)}) collective-permute-start(bf16[1,2,336,1536]{3,2,1,0:T(8,128)(2,1)} %bitcast.8), channel_id=1, source_target_pairs={{0,64},{64,0},{128,192},{192,128},{256,320},{320,256},{384,448},{4... | collective-permute-start | bytes 6193160 | tf_op jit(solution)/shard_map/ppermute | solution.py:212
  8.4 0.7 select_reduce_fusion.4
  9.2 0.2 reduce-window.15
  9.5 0.7 copy.20
  10.9 0.2 convolution_convert_fusion.q_ref
  11.1 0.4 collective-permute-done.far_ref
  11.5 0.6 collective-permute-done.1.near_ref
  12.1 1.2 shard_map.82
  13.3 29.3 %all_to_all.25.in_ref = bf16[8,416,128]{2,1,0:T(8,128)(2,1)S(1)} all-to-all(bf16[8,416,128]{2,1,0:T(8,128)(2,1)S(1)} %shard_map.82), channel_id=1, replica_groups={{0,128,256,384,512,640,768,896},{64,192,320,448,576,704,832,960},{1,129..., dimensions={0} | all-to-all | bytes 1703936 | tf_op jit(solution)/shard_map/all_to_all | solution.py:214
  42.7 4.7 %shard_map.83 = bf16[4,2,136,336]{3,2,1,0:T(8,128)(2,1)} custom-call(bf16[8,416,128]{2,1,0:T(8,128)(2,1)S(1)} %all_to_all.25.in_ref, bf16[1,2,336,1536]{3,2,1,0:T(8,128)(2,1)S(1)} %bitcast.9, bf16[1,2,336,1536]{3,2,1,0:T(8,128)(2,1)} %collective-permute-done.2.sib_w_ref), custom_call_target="tpu_custom_call" | custom-call | flops 1123024896 | tf_op jit(solution)/shard_map/pallas_call | solution.py:217
  47.3 7.3 %all-to-all-start.1 = ((bf16[4,2,136,336]{3,2,1,0:T(8,128)(2,1)}), bf16[4,2,136,336]{3,2,1,0:T(8,128)(2,1)S(1)}, u32[]{:S(2)}, u32[]{:S(2)}) async-start(bf16[4,2,136,336]{3,2,1,0:T(8,128)(2,1)} %shard_map.83), calls=%async_computation.1 | async-start | bytes 1671168 | tf_op jit(solution)/shard_map/all_to_all | solution.py:223
  54.6 1.9 %collective-permute-start.3 = (bf16[1,336,1536]{2,1,0:T(8,128)(2,1)S(1)}, bf16[1,336,1536]{2,1,0:T(8,128)(2,1)}, u32[]{:S(2)}, u32[]{:S(2)}) collective-permute-start(bf16[1,336,1536]{2,1,0:T(8,128)(2,1)S(1)} %bitcast.11), channel_id=1, source_target_pairs={{0,64},{64,0},{128,192},{192,128},{256,320},{320,256},{384,448},{4... | collective-permute-start | bytes 3096584 | tf_op jit(solution)/shard_map/ppermute | solution.py:213
  56.5 9.0 %all-to-all-done.1.in_ref = bf16[4,2,136,336]{3,2,1,0:T(8,128)(2,1)S(1)} async-done(((bf16[4,2,136,336]{3,2,1,0:T(8,128)(2,1)}), bf16[4,2,136,336]{3,2,1,0:T(8,128)(2,1)S(1)}, u32[]{:S(2)}, u32[]{:S(2)}) %all-to-all-start.1) | async-done | bytes 731168 | tf_op jit(solution)/shard_map/all_to_all | solution.py:223
  65.5 0.9 shard_map.84
  66.5 11.7 %all-to-all-start.2 = ((bf16[4,136,336]{2,1,0:T(8,128)(2,1)}), bf16[4,136,336]{2,1,0:T(8,128)(2,1)S(1)}, u32[]{:S(2)}, u32[]{:S(2)}) async-start(bf16[4,136,336]{2,1,0:T(8,128)(2,1)} %shard_map.84), calls=%async_computation.2 | async-start | bytes 835584 | tf_op jit(solution)/shard_map/all_to_all | solution.py:225
  78.1 6.4 %all-to-all-done.2.hid_ref = bf16[4,136,336]{2,1,0:T(8,128)(2,1)S(1)} async-done(((bf16[4,136,336]{2,1,0:T(8,128)(2,1)}), bf16[4,136,336]{2,1,0:T(8,128)(2,1)S(1)}, u32[]{:S(2)}, u32[]{:S(2)}) %all-to-all-start.2) | async-done | bytes 365600 | tf_op jit(solution)/shard_map/all_to_all | solution.py:225
  84.6 3.5 %shard_map.85 = bf16[8,416,128]{2,1,0:T(8,128)(2,1)} custom-call(bf16[4,136,336]{2,1,0:T(8,128)(2,1)S(1)} %all-to-all-done.2.hid_ref, bf16[1,336,1536]{2,1,0:T(8,128)(2,1)S(1)} %bitcast.12, bf16[1,336,1536]{2,1,0:T(8,128)(2,1)} %collective-permute-done.3.sib_w_ref), custom_call_target="tpu_custom_call" | custom-call | flops 561512448 | tf_op jit(solution)/shard_map/pallas_call | solution.py:226
  88.1 4.9 %all-to-all-start.3 = ((bf16[8,416,128]{2,1,0:T(8,128)(2,1)}), bf16[8,416,128]{2,1,0:T(8,128)(2,1)S(1)}, u32[]{:S(2)}, u32[]{:S(2)}) async-start(bf16[8,416,128]{2,1,0:T(8,128)(2,1)} %shard_map.85), calls=%async_computation.3 | async-start | bytes 1703936 | tf_op jit(solution)/shard_map/all_to_all | solution.py:231
  93.4 16.4 %all-to-all-done.3.in_ref = bf16[8,416,128]{2,1,0:T(8,128)(2,1)S(1)} async-done(((bf16[8,416,128]{2,1,0:T(8,128)(2,1)}), bf16[8,416,128]{2,1,0:T(8,128)(2,1)S(1)}, u32[]{:S(2)}, u32[]{:S(2)}) %all-to-all-start.3) | async-done | bytes 852000 | tf_op jit(solution)/shard_map/all_to_all | solution.py:231
  109.9 0.5 shard_map.86
  110.3 38.5 %all_to_all.26 = bf16[16,8,1536]{2,1,0:T(8,128)(2,1)S(1)} all-to-all(bf16[16,8,1536]{2,1,0:T(8,128)(2,1)S(1)} %bitcast.10), channel_id=1, replica_groups=mesh['seq'=16,'exp'=16,'rep'=4] {'exp'}, dimensions={0} | all-to-all | bytes 786432 | tf_op jit(solution)/shard_map/all_to_all | solution.py:238
  148.8 0.7 reduce_sum.52
  (33 shorter events, 1.4 us)
Async XLA Ops:
  0.0 10.9 %copy-start = (bf16[128,6144]{1,0:T(8,128)(2,1)S(1)}, bf16[128,6144]{1,0:T(8,128)(2,1)}, u32[]{:S(2)}) copy-start(bf16[128,6144]{1,0:T(8,128)(2,1)} %param.8) | copy-start | bytes 4718596
  1.0 10.5 %collective-permute-start = (bf16[128,512]{1,0:T(8,128)(2,1)S(1)}, bf16[128,512]{1,0:T(8,128)(2,1)S(1)}, u32[]{:S(2)}, u32[]{:S(2)}) collective-permute-start(bf16[128,512]{1,0:T(8,128)(2,1)S(1)} %pad_maximum_fusion.own_ref), channel_id=1, source_target_pairs={{0,128},{64,192},{128,256},{192,320},{256,384},{320,448},{384,512}... | collective-permute-start | bytes 393224 | tf_op jit(solution)/shard_map/ppermute | solution.py:183
  4.6 7.5 %collective-permute-start.1 = (bf16[128,512]{1,0:T(8,128)(2,1)S(1)}, bf16[128,512]{1,0:T(8,128)(2,1)S(1)}, u32[]{:S(2)}, u32[]{:S(2)}) collective-permute-start(bf16[128,512]{1,0:T(8,128)(2,1)S(1)} %pad_maximum_fusion.own_ref), channel_id=1, source_target_pairs={{0,64},{64,128},{128,192},{192,256},{256,320},{320,384},{384,448},... | collective-permute-start | bytes 393224 | tf_op jit(solution)/shard_map/ppermute | solution.py:184
  4.7 38.0 %collective-permute-start.2 = (bf16[1,2,336,1536]{3,2,1,0:T(8,128)(2,1)}, bf16[1,2,336,1536]{3,2,1,0:T(8,128)(2,1)}, u32[]{:S(2)}, u32[]{:S(2)}) collective-permute-start(bf16[1,2,336,1536]{3,2,1,0:T(8,128)(2,1)} %bitcast.8), channel_id=1, source_target_pairs={{0,64},{64,0},{128,192},{192,128},{256,320},{320,256},{384,448},{4... | collective-permute-start | bytes 6193160 | tf_op jit(solution)/shard_map/ppermute | solution.py:212
  11.1 31.5 %copy-start.1 = (bf16[1,1536,2,336]{1,3,2,0:T(8,128)(2,1)S(1)}, bf16[1,1536,2,336]{1,3,2,0:T(8,128)(2,1)}, u32[]{:S(2)}) copy-start(bf16[1,1536,2,336]{1,3,2,0:T(8,128)(2,1)} %param.14) | copy-start | bytes 6193156
  47.3 7.3 %copy-start.2 = (bf16[1,1536,336]{1,2,0:T(8,128)(2,1)S(1)}, bf16[1,1536,336]{1,2,0:T(8,128)(2,1)}, u32[]{:S(2)}) copy-start(bf16[1,1536,336]{1,2,0:T(8,128)(2,1)} %param.15) | copy-start | bytes 3096580
  47.3 18.2 %all-to-all-start.1 = ((bf16[4,2,136,336]{3,2,1,0:T(8,128)(2,1)}), bf16[4,2,136,336]{3,2,1,0:T(8,128)(2,1)S(1)}, u32[]{:S(2)}, u32[]{:S(2)}) async-start(bf16[4,2,136,336]{3,2,1,0:T(8,128)(2,1)} %shard_map.83), calls=%async_computation.1 | async-start | bytes 1671168 | tf_op jit(solution)/shard_map/all_to_all | solution.py:223
  54.6 23.5 %collective-permute-start.3 = (bf16[1,336,1536]{2,1,0:T(8,128)(2,1)S(1)}, bf16[1,336,1536]{2,1,0:T(8,128)(2,1)}, u32[]{:S(2)}, u32[]{:S(2)}) collective-permute-start(bf16[1,336,1536]{2,1,0:T(8,128)(2,1)S(1)} %bitcast.11), channel_id=1, source_target_pairs={{0,64},{64,0},{128,192},{192,128},{256,320},{320,256},{384,448},{4... | collective-permute-start | bytes 3096584 | tf_op jit(solution)/shard_map/ppermute | solution.py:213
  66.5 18.1 %all-to-all-start.2 = ((bf16[4,136,336]{2,1,0:T(8,128)(2,1)}), bf16[4,136,336]{2,1,0:T(8,128)(2,1)S(1)}, u32[]{:S(2)}, u32[]{:S(2)}) async-start(bf16[4,136,336]{2,1,0:T(8,128)(2,1)} %shard_map.84), calls=%async_computation.2 | async-start | bytes 835584 | tf_op jit(solution)/shard_map/all_to_all | solution.py:225
  88.1 21.8 %all-to-all-start.3 = ((bf16[8,416,128]{2,1,0:T(8,128)(2,1)}), bf16[8,416,128]{2,1,0:T(8,128)(2,1)S(1)}, u32[]{:S(2)}, u32[]{:S(2)}) async-start(bf16[8,416,128]{2,1,0:T(8,128)(2,1)} %shard_map.85), calls=%async_computation.3 | async-start | bytes 1703936 | tf_op jit(solution)/shard_map/all_to_all | solution.py:231

commit v3 on v2

--- a/solution.py
+++ b/solution.py
@@ -28,10 +28,12 @@
     return lax.broadcasted_iota(jnp.int32, shape, dim)
 
 
-def attend_kernel(heads, kv_heads, q_ref, far_ref, near_ref, own_ref, low_ref, high_ref, out_ref):
+def attend_kernel(heads, kv_heads, q_ref, far_ref, near_ref, own_ref, low_ref, high_ref, share_in, left_in, out_ref, share_ref, left_ref):
+    share_ref[...] = share_in[...]
+    left_ref[...] = left_in[...]
     group = heads // kv_heads
     rows = group * SLOTS
-    left_rows = out_ref.shape[1] - heads * MAIN
+    left_rows = out_ref.shape[0] - heads * MAIN
     keys_in = (REACH + 1) * own_ref.shape[0]
     key_at = iota((rows, keys_in), 1)
     allowed = (key_at >= low_ref[...]) & (key_at <= high_ref[...])
@@ -49,17 +51,13 @@
         mixed = dot(probs, v).astype(BF)
         for j in range(group):
             head = g * group + j
-            part = mixed[j * SLOTS : j * SLOTS + MAIN]
-            for y in range(out_ref.shape[0]):
-                out_ref[y, head * MAIN : (head + 1) * MAIN, :] = part
+            out_ref[head * MAIN : (head + 1) * MAIN, :] = mixed[j * SLOTS : j * SLOTS + MAIN]
         at = iota((left_rows, rows), 0) - g * group * LEFT
         col = iota((left_rows, rows), 1)
         wanted = (at >> 1) * SLOTS + MAIN + (at & 1)
         pick = ((col == wanted) & (at >= 0) & (at < group * LEFT)).astype(F32).astype(BF)
         left = left + dot(pick, mixed)
-    left = left.astype(BF)
-    for y in range(out_ref.shape[0]):
-        out_ref[y, heads * MAIN :, :] = left
+    out_ref[heads * MAIN :, :] = left.astype(BF)
 
 
 def left_index(shape, heads, blocks, left_rows, row_dim):
@@ -70,15 +68,23 @@
     return (col == (inside >> 1) * left_rows + head * LEFT + (inside & 1)).astype(F32).astype(BF)
 
 
-def own_of(shape, row_dim, n, per):
-    row, col = iota(shape, row_dim), iota(shape, 1 - row_dim)
-    chunk = row // (2 * per)
-    inside = row - chunk * 2 * per
-    shard = inside // per
-    return (col == shard * n * per + chunk * per + inside - shard * per).astype(F32).astype(BF)
-
-
-def gate_kernel(heads, in_ref, own_w_ref, sib_w_ref, out_ref, x_ref):
+def joined(own, sib, start, stop):
+    n = own.shape[0]
+    parts = []
+    if start < n:
+        parts.append(own[start : min(stop, n)])
+    if stop > n:
+        parts.append(sib[max(start - n, 0) : stop - n])
+    return parts[0] if len(parts) == 1 else jnp.concatenate(parts, 0)
+
+
+def silu_times(gate, up):
+    return gate / (1.0 + jnp.exp(-gate)) * up
+
+
+def gate_kernel(heads, in_ref, own_w_ref, far_w_ref, out_ref, x_ref, sib_w_ref, sem):
+    fetch = pltpu.make_async_copy(far_w_ref, sib_w_ref, sem)
+    fetch.start()
     blocks, flat, _ = in_ref.shape
     chunks = out_ref.shape[0]
     left_rows = flat - heads * MAIN
@@ -91,23 +97,69 @@
     for h in range(heads):
         x_ref[main:, h * HD : (h + 1) * HD] = left[h * extra : (h + 1) * extra]
     x = x_ref[...]
-    order = own_of((2 * extra, 2 * extra), 0, chunks, n)
-    for part in range(2):
-        own = lax.dot_general(x, own_w_ref[0, part], NT, preferred_element_type=F32)
-        sib = lax.dot_general(x, sib_w_ref[0, part], NT, preferred_element_type=F32)
-        left = dot(order, jnp.concatenate([own[main:], sib[main:]], 0).astype(BF))
-        for j in range(chunks):
-            rows = [own[j * m : (j + 1) * m], sib[j * m : (j + 1) * m], left[j * 2 * n : (j + 1) * 2 * n]]
-            out_ref[j, part] = jnp.concatenate(rows, 0).astype(BF)
-
-
-def hidden_kernel(in_ref, out_ref):
-    n = in_ref.shape[0]
-    gate = sum(in_ref[i, 0].astype(F32) for i in range(n))
-    up = sum(in_ref[i, 1].astype(F32) for i in range(n))
-    hidden = (gate / (1.0 + jnp.exp(-gate)) * up).astype(BF)
-    for i in range(n):
-        out_ref[i] = hidden
+    full = 2 * own_w_ref.shape[2] // HD
+
+    def times(*w):
+        w = w[0] if len(w) == 1 else jnp.concatenate(w, 0)
+        return lax.dot_general(x, w, NT, preferred_element_type=F32)
+
+    def units(part, start, stop):
+        return joined(own_w_ref.at[0, part], sib_w_ref.at[0, part], start, stop)
+
+    tiles = [[], []]
+    for t in range(0, full - 1, 2):
+        if t == 2:
+            fetch.wait()
+        for part in range(2):
+            both = times(units(part, t * HD, (t + 2) * HD))
+            tiles[part] += [both[:, :HD], both[:, HD:]]
+    both = times(*(units(part, (full - 1) * HD, full * HD) for part in range(2)))
+    tiles[0].append(both[:, :HD])
+    tiles[1].append(both[:, HD:])
+    rest = [units(part, full * HD, full * HD + HD // 4) for part in range(2)]
+    rest = times(*rest, *rest)
+    tiles = tiles[0] + tiles[1]
+    packed = 2 * full * m + m // 2
+    stack = jnp.concatenate([t[main:] for t in tiles + [rest]], 0).astype(BF)
+    per = out_ref.shape[1] - packed
+    row, col = iota((chunks * per, stack.shape[0]), 0), iota((chunks * per, stack.shape[0]), 1)
+    chunk = row // per
+    inside = row - chunk * per
+    t, up, i = inside // (2 * n), (inside // n) & 1, inside & (n - 1)
+    wanted = jnp.where(t < full, (up * full + t) * extra, jnp.where(up == 0, 2 * full * extra, -stack.shape[0]))
+    order = (col == wanted + chunk * n + i).astype(F32).astype(BF)
+    left = dot(order, stack).astype(BF)
+    first = iota((m // 2, HD), 1) < HD // 2
+    for j in range(chunks):
+        for k, tile in enumerate(tiles):
+            out_ref[j, k * m : (k + 1) * m, :] = tile[j * m : (j + 1) * m].astype(BF)
+        pair = jnp.where(first, rest[j * m : j * m + m // 2], rest[j * m + m // 2 : (j + 1) * m])
+        out_ref[j, 2 * full * m : packed, :] = pair.astype(BF)
+        out_ref[j, packed:, :] = left[j * per : (j + 1) * per]
+
+
+def hidden_kernel(full, m, n, in_ref, out_ref):
+    both = sum(in_ref[i].astype(F32) for i in range(in_ref.shape[0]))
+    tall, packed = full * m, 2 * full * m + m // 2
+    quarter = HD // 4
+
+    def rest(x):
+        return silu_times(x, pltpu.roll(x, HD - quarter, 1))
+
+    main = silu_times(both[:tall], both[tall : 2 * tall])
+    pair = both[2 * tall : packed]
+    pair = jnp.where((iota(pair.shape, 1) & (2 * quarter - 1)) < quarter, rest(pair), 0.0)
+    left = both[packed : packed + 2 * n * full]
+    left = silu_times(left, pltpu.roll(left, left.shape[0] - n, 0))
+    last = both[packed + 2 * n * full :]
+    last = jnp.where(iota(last.shape, 1) < quarter, rest(last), 0.0)
+    left = jnp.concatenate([left, last], 0).astype(BF)
+    rows = out_ref.shape[0] - tall - m // 2
+    row, col = iota((rows, left.shape[0]), 0), iota((rows, left.shape[0]), 1)
+    pick = ((col == row // n * 2 * n + (row & (n - 1))) & (row < n * (full + 1))).astype(F32).astype(BF)
+    out_ref[:tall, :] = main.astype(BF)
+    out_ref[tall : tall + m // 2, :] = pair.astype(BF)
+    out_ref[tall + m // 2 :, :] = dot(pick, left).astype(BF)
 
 
 def down_kernel(heads, hid_ref, own_w_ref, sib_w_ref, out_ref):
@@ -117,12 +169,37 @@
     main, extra = blocks * MAIN, blocks * LEFT
     m, n = main // chunks, extra // chunks
     put = left_index((blocks * left_rows, heads * extra), heads, blocks, left_rows, 1)
-    held = [hid_ref[j].astype(F32) for j in range(chunks)]
-    order = own_of((2 * extra, 2 * extra), 1, chunks, n)
-    left = dot(order, jnp.concatenate([c[2 * m :] for c in held], 0).astype(BF))
-    own = jnp.concatenate([c[:m] for c in held] + [left[:extra]], 0).astype(BF)
-    sib = jnp.concatenate([c[m : 2 * m] for c in held] + [left[extra:]], 0).astype(BF)
-    out = (dot(own, own_w_ref[0]) + dot(sib, sib_w_ref[0])).astype(BF)
+    full = 2 * own_w_ref.shape[1] // HD
+    tall = full * m
+    rest_rows = hid_ref.shape[1] - tall - m // 2
+    tiles = [jnp.concatenate([hid_ref[j, t * m : (t + 1) * m, :] for j in range(chunks)], 0) for t in range(full)]
+    first = iota((m // 2, HD), 1) < HD // 2
+    pairs = []
+    for j in range(chunks):
+        pair = hid_ref[j, tall : tall + m // 2, :].astype(F32)
+        pairs += [jnp.where(first, pair, 0.0), jnp.where(first, 0.0, pair)]
+    tiles.append(jnp.concatenate(pairs, 0).astype(BF))
+    stack = jnp.concatenate([hid_ref[j, tall + m // 2 :, :] for j in range(chunks)], 0)
+    shape = ((full + 1) * extra, stack.shape[0])
+    row, col = iota(shape, 0), iota(shape, 1)
+    t = row // extra
+    inside = row - t * extra
+    order = (col == inside // n * rest_rows + t * n + (inside & (n - 1))).astype(F32).astype(BF)
+    left = dot(order, stack).astype(BF)
+    hidden = [jnp.concatenate([tile, left[t * extra : (t + 1) * extra]], 0) for t, tile in enumerate(tiles)]
+
+    def units(start, stop):
+        return joined(own_w_ref.at[0], sib_w_ref.at[0], start, stop)
+
+    out = None
+    for t in range(0, full + 1, 2):
+        if t + 2 <= full:
+            w = units(t * HD, (t + 2) * HD)
+        else:
+            w = jnp.concatenate([units(t * HD, full * HD)] + [units(full * HD, full * HD + HD // 4)] * 4, 0)
+        term = dot(jnp.concatenate(hidden[t : t + 2], 1), w)
+        out = term if out is None else out + term
+    out = out.astype(BF)
     for h in range(heads):
         out_ref[:, h * MAIN : (h + 1) * MAIN, :] = out[:main, h * HD : (h + 1) * HD].reshape(blocks, MAIN, HD)
     stack = jnp.concatenate([out[main:, h * HD : (h + 1) * HD] for h in range(heads)], 0)
@@ -148,12 +225,16 @@
     out_ref[...] = dot(put_ref[...], x_ref[...]).astype(BF)
 
 
-def call(kernel, shapes, scratch=(), flops=0, moved=0):
+def call(kernel, shapes, scratch=(), flops=0, moved=0, in_hbm=None):
+    spaces = {}
+    if in_hbm is not None:
+        spaces["in_specs"] = [pl.BlockSpec(memory_space=pl.ANY if at == in_hbm[0] else pltpu.VMEM) for at in range(in_hbm[1])]
     return pl.pallas_call(
         kernel,
+        **spaces,
         out_shape=shapes,
         scratch_shapes=list(scratch),
-        compiler_params=pltpu.CompilerParams(vmem_limit_bytes=48 * 1024 * 1024),
+        compiler_params=pltpu.CompilerParams(vmem_limit_bytes=12 * 1024 * 1024),
         cost_estimate=pl.CostEstimate(flops=flops, bytes_accessed=moved, transcendentals=0),
     )
 
@@ -201,28 +282,39 @@
     q_cols = lax.dynamic_slice_in_dim(queries, rep_at * cols, cols, 1)
     q_rows = dot(pick.astype(BF), q_cols).astype(BF)
 
-    spread = call(
+    spread, share, left_share = call(
         functools.partial(attend_kernel, heads, kv_heads),
-        jax.ShapeDtypeStruct((n_y, flat, HD), BF),
+        [
+            jax.ShapeDtypeStruct((flat, HD), BF),
+            jax.ShapeDtypeStruct((MAIN, 1), F32),
+            jax.ShapeDtypeStruct((left_rows, 1), F32),
+        ],
         flops=4 * heads * SLOTS * 3 * tok * HD,
-    )(q_rows, far, near, kv, jnp.tile(low, group)[:, None], jnp.tile(high, group)[:, None])
+    )(q_rows, far, near, kv, jnp.tile(low, group)[:, None], jnp.tile(high, group)[:, None], share[:MAIN, None], left_share[:, None])
 
     gate_w = jnp.transpose(gate_up, (0, 2, 3, 1))
     down_w = jnp.transpose(down_t, (0, 2, 1))
     sib_gate_w = lax.ppermute(gate_w, "seq", sibling)
     sib_down_w = lax.ppermute(down_w, "seq", sibling)
-    mine = lax.all_to_all(spread, "seq", split_axis=0, concat_axis=0, tiled=True, axis_index_groups=same_core)
-
-    rows = 2 * n_y * CAP // n_rep
+    mine = lax.all_gather(spread, "seq", axis_index_groups=same_core)
+    mine, sib_gate_w, sib_down_w, put = lax.optimization_barrier(
+        (mine, sib_gate_w, sib_down_w, put)
+    )
+
+    full = 2 * hid // HD
+    m, n = n_y * MAIN // n_rep, n_y * LEFT // n_rep
+    part_rows = 2 * full * m + m // 2 + 2 * n * (full + 1)
+    hid_rows = -(-(full * m + m // 2 + n * (full + 1)) // 16) * 16
     parts = call(
         functools.partial(gate_kernel, heads),
-        jax.ShapeDtypeStruct((n_rep, 2, rows, hid), BF),
-        [pltpu.VMEM((n_y * CAP, cols), BF)],
+        jax.ShapeDtypeStruct((n_rep, part_rows, HD), BF),
+        [pltpu.VMEM((n_y * CAP, cols), BF), pltpu.VMEM(gate_w.shape, BF), pltpu.SemaphoreType.DMA],
         flops=8 * n_y * CAP * cols * hid,
+        in_hbm=(2, 3),
     )(mine, gate_w, sib_gate_w)
     parts = lax.all_to_all(parts, "rep", split_axis=0, concat_axis=0, tiled=True)
-    hidden = call(hidden_kernel, jax.ShapeDtypeStruct((n_rep, rows, hid), BF))(parts)
-    hidden = lax.all_to_all(hidden, "rep", split_axis=0, concat_axis=0, tiled=True)
+    hidden = call(functools.partial(hidden_kernel, full, m, n), jax.ShapeDtypeStruct((hid_rows, HD), BF))(parts)
+    hidden = lax.all_gather(hidden, "rep")
     mine = call(
         functools.partial(down_kernel, heads),
         jax.ShapeDtypeStruct((n_y, flat, HD), BF),
@@ -234,7 +326,7 @@
         jax.ShapeDtypeStruct((tok, cols), BF),
         [pltpu.VMEM((SLOTS, cols), BF)],
         flops=2 * SLOTS * tok * cols,
-    )(mine, put, share[:MAIN, None], left_share[:, None])
+    )(mine, put, share, left_share)
     terms = lax.all_to_all(term.reshape(n_exp, tok // n_exp, cols), "exp", split_axis=0, concat_axis=0, tiled=True)
     return jnp.sum(terms.astype(F32), axis=0).astype(BF)
 

time: 150 us -> 137 us (0.913)
  blocking collectives: 67.8 us -> 116 us
  waiting for transfers between devices: 32.8 us -> 0.01 us
  starting transfers between devices: 33.1 us -> 8.95 us
  Pallas kernels: 10.8 us -> 5.81 us
    all_gather x0 -> x2, blocking collectives: none -> 43.1 us  [the longest x1 27.7 us: per_device(): mine = lax.all_gather(spread, 'seq', axis_index_groups=same_core)]
    all_to_all x3 -> x0, waiting for transfers between devices: 31.9 us -> none  [the longest x1 16.4 us: per_device(): lax.all_to_all(mine, 'seq', split_axis=0, concat_axis=0, tiled=True, axis...]
    all_to_all x3 -> x0, starting transfers between devices: 23.9 us -> none  [the longest x1 11.7 us: per_device(): lax.all_to_all(hidden, 'rep', split_axis=0, concat_axis=0, tiled=True)]
    all_to_all x1 -> x2, blocking collectives: 29.3 us -> 45.7 us  [the longest x1 25.3 us: per_device(): lax.all_to_all(parts, 'rep', split_axis=0, concat_axis=0, tiled=True)]
    all_to_all x1, blocking collectives: 38.5 us -> 27.5 us  [per_device(): lax.all_to_all(term.reshape(n_exp, tok // n_exp, cols), 'exp', split_axis...]
    pallas_call x1, Pallas kernels: 3.48 us -> 1.03 us  [per_device(): call(functools.partial(down_kernel, heads), jax.ShapeDtypeStruct((n_y, fl...]
    pallas_call x1, Pallas kernels: 4.69 us -> 2.9 us  [per_device(): call(functools.partial(gate_kernel, heads), jax.ShapeDtypeStruct((n_rep,...]
    ppermute x1, starting transfers between devices: 3.69 us -> 1.92 us  [per_device(): sib_gate_w = lax.ppermute(gate_w, 'seq', sibling)]
  transfers between devices with their start and end apart: 7 -> 4, of which waited for: 5 -> 0; matrix products, arithmetic and copies ran while one was open for 2% -> 2% of each run, Pallas kernels for 1% -> 1%
where the time goes in v3:
time: 137 us; the launch traced here: 136 us
  blocking collectives  116 us (85%)
  starting transfers between devices  8.95 us (7%)
  Pallas kernels  5.81 us (4%)
  local copies, waits for them, and re-layouts  2.36 us (2%)
  other arithmetic  2.26 us (2%)
    all_gather x1, blocking collectives, per_device(): mine = lax.all_gather(spread, 'seq', axis_index_groups=same_core)  27.7 us
    all_to_all x1, blocking collectives, per_device(): lax.all_to_all(term.reshape(n_exp, tok // n_exp, cols), 'exp', split_axis...  27.5 us
    all_to_all x1, blocking collectives, per_device(): lax.all_to_all(parts, 'rep', split_axis=0, concat_axis=0, tiled=True)  25.3 us
    all_to_all x1, blocking collectives, per_device(): lax.all_to_all(mine, 'seq', split_axis=0, concat_axis=0, tiled=True, axis...  20.4 us
    all_gather x1, blocking collectives, per_device(): hidden = lax.all_gather(hidden, 'rep')  15.4 us
    ppermute x1, starting transfers between devices, per_device(): far = lax.ppermute(kv, 'seq', [(i, (i + 2) % n_seq) for i in range(n_seq)])  3.6 us
    ppermute x1, starting transfers between devices, per_device(): sib_down_w = lax.ppermute(down_w, 'seq', sibling)  3.41 us
    pallas_call x1, Pallas kernels, per_device(): call(functools.partial(gate_kernel, heads), jax.ShapeDtypeStruct((n_rep,...  2.9 us
  transfers between devices with their start and end apart: 4, of which 0 were waited for; matrix products, arithmetic and copies ran while one was open for 2% of the time, Pallas kernels for 1%

profile of v3, /device:TPU:14, one launch (start us, length us, event | category | flops | bytes accessed | tf_op | source)
XLA Modules:
  0.0 136.1 jit_solution(2387622928088542064)
XLA Ops:
  0.0 1.0 constant_dynamic-slice_fusion
  1.1 3.6 %collective-permute-start = (bf16[128,512]{1,0:T(8,128)(2,1)S(1)}, bf16[128,512]{1,0:T(8,128)(2,1)S(1)}, u32[]{:S(2)}, u32[]{:S(2)}) collective-permute-start(bf16[128,512]{1,0:T(8,128)(2,1)S(1)} %pad_maximum_fusion.own_ref), channel_id=1, source_target_pairs={{0,128},{64,192},{128,256},{192,320},{256,384},{320,448},{384,512}... | collective-permute-start | bytes 393224 | tf_op jit(solution)/shard_map/ppermute | solution.py:264
  4.7 3.4 %collective-permute-start.3 = (bf16[1,336,1536]{2,1,0:T(8,128)(2,1)}, bf16[1,336,1536]{2,1,0:T(8,128)(2,1)S(1)}, u32[]{:S(2)}, u32[]{:S(2)}) collective-permute-start(bf16[1,336,1536]{2,1,0:T(8,128)(2,1)} %bitcast.15), channel_id=1, source_target_pairs={{0,64},{64,0},{128,192},{192,128},{256,320},{320,256},{384,448},{4... | collective-permute-start | bytes 3096584 | tf_op jit(solution)/shard_map/ppermute | solution.py:298
  8.1 1.9 %collective-permute-start.2 = (bf16[1,2,336,1536]{3,2,1,0:T(8,128)(2,1)}, bf16[1,2,336,1536]{3,2,1,0:T(8,128)(2,1)}, u32[]{:S(2)}, u32[]{:S(2)}) collective-permute-start(bf16[1,2,336,1536]{3,2,1,0:T(8,128)(2,1)} %bitcast.11), channel_id=1, source_target_pairs={{0,64},{64,0},{128,192},{192,128},{256,320},{320,256},{384,448},{4... | collective-permute-start | bytes 6193160 | tf_op jit(solution)/shard_map/ppermute | solution.py:297
  10.0 0.7 select_reduce_fusion.4
  10.8 0.1 copy.19
  10.9 0.2 reduce-window.15
  11.2 0.7 copy.20
  11.9 0.1 reduce.2
  12.5 0.1 select_reduce_fusion.1
  12.7 0.1 broadcast_in_dim_tile.12.low_ref
  12.8 0.1 broadcast_in_dim_tile.13.high_ref
  12.9 0.2 convolution_convert_fusion.q_ref
  13.3 1.2 shard_map.82
  14.5 27.7 %all-gather = bf16[3328,128]{1,0:T(8,128)(2,1)S(1)} all-gather(bf16[416,128]{1,0:T(8,128)(2,1)S(1)} %get-tuple-element.12), channel_id=2, replica_groups={{0,128,256,384,512,640,768,896},{64,192,320,448,576,704,832,960},{1,129..., dimensions={0}, use_global_device_ids=true | all-gather | bytes 958464 | tf_op jit(solution)/shard_map/all_gather | solution.py:299
  42.2 2.9 %shard_map.83 = bf16[4,720,128]{2,1,0:T(8,128)(2,1)S(1)} custom-call(bf16[8,416,128]{2,1,0:T(8,128)(2,1)S(1)} %bitcast.10, bf16[1,2,336,1536]{3,2,1,0:T(8,128)(2,1)S(1)} %bitcast.12, bf16[1,2,336,1536]{3,2,1,0:T(8,128)(2,1)} %collective-permute-done.2.far_w_ref), custom_call_target="tpu_custom_call" | custom-call | flops 1123024896 | tf_op jit(solution)/shard_map/pallas_call | solution.py:308
  45.1 25.3 %all_to_all.15.in_ref = bf16[4,720,128]{2,1,0:T(8,128)(2,1)S(1)} all-to-all(bf16[4,720,128]{2,1,0:T(8,128)(2,1)S(1)} %shard_map.83), channel_id=1, replica_groups=mesh['seq'=16,'exp'=16,'rep'=4] {'rep'}, dimensions={0} | all-to-all | bytes 1474560 | tf_op jit(solution)/shard_map/all_to_all | solution.py:315
  70.4 0.2 shard_map.84
  70.7 15.4 %all-gather.1 = bf16[1536,128]{1,0:T(8,128)(2,1)S(1)} all-gather(bf16[384,128]{1,0:T(8,128)(2,1)S(1)} %shard_map.84), channel_id=3, replica_groups=mesh['seq'=16,'exp'=16,'rep'=4] {'rep'}, dimensions={0}, use_global_device_ids=true | all-gather | bytes 491520 | tf_op jit(solution)/shard_map/all_gather | solution.py:317
  86.0 1.0 shard_map.85
  87.1 20.4 %all_to_all.16.in_ref = bf16[8,416,128]{2,1,0:T(8,128)(2,1)S(1)} all-to-all(bf16[8,416,128]{2,1,0:T(8,128)(2,1)S(1)} %shard_map.85), channel_id=1, replica_groups={{0,128,256,384,512,640,768,896},{64,192,320,448,576,704,832,960},{1,129..., dimensions={0} | all-to-all | bytes 1703936 | tf_op jit(solution)/shard_map/all_to_all | solution.py:323
  107.4 0.5 shard_map.86
  107.9 27.5 %all_to_all.17 = bf16[16,8,1536]{2,1,0:T(8,128)(2,1)S(1)} all-to-all(bf16[16,8,1536]{2,1,0:T(8,128)(2,1)S(1)} %bitcast.14), channel_id=1, replica_groups=mesh['seq'=16,'exp'=16,'rep'=4] {'exp'}, dimensions={0} | all-to-all | bytes 786432 | tf_op jit(solution)/shard_map/all_to_all | solution.py:330
  135.4 0.7 reduce_sum.52
  (30 shorter events, 0.8 us)
Async XLA Ops:
  0.0 12.9 %copy-start = (bf16[128,6144]{1,0:T(8,128)(2,1)S(1)}, bf16[128,6144]{1,0:T(8,128)(2,1)}, u32[]{:S(2)}) copy-start(bf16[128,6144]{1,0:T(8,128)(2,1)} %param.8) | copy-start | bytes 4718596
  1.0 12.2 %collective-permute-start.1 = (bf16[128,512]{1,0:T(8,128)(2,1)S(1)}, bf16[128,512]{1,0:T(8,128)(2,1)S(1)}, u32[]{:S(2)}, u32[]{:S(2)}) collective-permute-start(bf16[128,512]{1,0:T(8,128)(2,1)S(1)} %pad_maximum_fusion.own_ref), channel_id=1, source_target_pairs={{0,64},{64,128},{128,192},{192,256},{256,320},{320,384},{384,448},... | collective-permute-start | bytes 393224 | tf_op jit(solution)/shard_map/ppermute | solution.py:265
  1.1 12.2 %collective-permute-start = (bf16[128,512]{1,0:T(8,128)(2,1)S(1)}, bf16[128,512]{1,0:T(8,128)(2,1)S(1)}, u32[]{:S(2)}, u32[]{:S(2)}) collective-permute-start(bf16[128,512]{1,0:T(8,128)(2,1)S(1)} %pad_maximum_fusion.own_ref), channel_id=1, source_target_pairs={{0,128},{64,192},{128,256},{192,320},{256,384},{320,448},{384,512}... | collective-permute-start | bytes 393224 | tf_op jit(solution)/shard_map/ppermute | solution.py:264
  4.7 37.5 %collective-permute-start.3 = (bf16[1,336,1536]{2,1,0:T(8,128)(2,1)}, bf16[1,336,1536]{2,1,0:T(8,128)(2,1)S(1)}, u32[]{:S(2)}, u32[]{:S(2)}) collective-permute-start(bf16[1,336,1536]{2,1,0:T(8,128)(2,1)} %bitcast.15), channel_id=1, source_target_pairs={{0,64},{64,0},{128,192},{192,128},{256,320},{320,256},{384,448},{4... | collective-permute-start | bytes 3096584 | tf_op jit(solution)/shard_map/ppermute | solution.py:298
  8.1 34.1 %collective-permute-start.2 = (bf16[1,2,336,1536]{3,2,1,0:T(8,128)(2,1)}, bf16[1,2,336,1536]{3,2,1,0:T(8,128)(2,1)}, u32[]{:S(2)}, u32[]{:S(2)}) collective-permute-start(bf16[1,2,336,1536]{3,2,1,0:T(8,128)(2,1)} %bitcast.11), channel_id=1, source_target_pairs={{0,64},{64,0},{128,192},{192,128},{256,320},{320,256},{384,448},{4... | collective-permute-start | bytes 6193160 | tf_op jit(solution)/shard_map/ppermute | solution.py:297
  12.9 29.3 %copy-start.1 = (bf16[1,1536,2,336]{1,3,2,0:T(8,128)(2,1)S(1)}, bf16[1,1536,2,336]{1,3,2,0:T(8,128)(2,1)}, u32[]{:S(2)}) copy-start(bf16[1,1536,2,336]{1,3,2,0:T(8,128)(2,1)} %param.14) | copy-start | bytes 6193156
  45.1 40.9 %copy-start.2 = (bf16[1,1536,336]{1,2,0:T(8,128)(2,1)S(1)}, bf16[1,1536,336]{1,2,0:T(8,128)(2,1)}, u32[]{:S(2)}) copy-start(bf16[1,1536,336]{1,2,0:T(8,128)(2,1)} %param.15) | copy-start | bytes 3096580

commit v4 on v3

--- a/solution.py
+++ b/solution.py
@@ -28,15 +28,28 @@
     return lax.broadcasted_iota(jnp.int32, shape, dim)
 
 
-def attend_kernel(heads, kv_heads, q_ref, far_ref, near_ref, own_ref, low_ref, high_ref, share_in, left_in, out_ref, share_ref, left_ref):
-    share_ref[...] = share_in[...]
-    left_ref[...] = left_in[...]
+def attend_kernel(heads, kv_heads, q_ref, far_ref, near_ref, own_ref, slot_ref, low_ref, share_in, out_ref, put_ref, share_ref, left_ref):
+    tok = own_ref.shape[0]
+    pick = (slot_ref[...] == iota((SLOTS, tok), 0)).astype(F32)
+
+    def of_slot(row):
+        return jnp.sum(pick * row, axis=1, keepdims=True)
+
+    low = of_slot(low_ref[...].astype(F32)).astype(jnp.int32)
+    high = of_slot(iota((1, tok), 1).astype(F32)).astype(jnp.int32) + REACH * tok
+    share = of_slot(share_in[...])
+    share_ref[...] = share[:MAIN]
+    odd = iota(left_ref.shape, 0) & 1
+    left_ref[...] = jnp.where(odd == 0, share[MAIN : MAIN + 1], share[MAIN + 1 : MAIN + 2])
+    same = (iota((tok, tok), 0) == iota((tok, tok), 1)).astype(F32).astype(BF)
+    put_ref[...] = lax.dot_general(same, pick.astype(BF), NT, preferred_element_type=F32).astype(BF)
     group = heads // kv_heads
     rows = group * SLOTS
     left_rows = out_ref.shape[0] - heads * MAIN
     keys_in = (REACH + 1) * own_ref.shape[0]
     key_at = iota((rows, keys_in), 1)
-    allowed = (key_at >= low_ref[...]) & (key_at <= high_ref[...])
+    low, high = (jnp.concatenate([bound] * group, 0) for bound in (low, high))
+    allowed = (key_at >= low) & (key_at <= high)
     left = jnp.zeros((left_rows, HD), F32)
     for g in range(kv_heads):
         k_cols = slice(g * HD, (g + 1) * HD)
@@ -270,36 +283,30 @@
     rank = jnp.cumsum(match) - match
     slot = jnp.where(match > 0, rank, -1)
     pick = slot[None, :] == jnp.arange(SLOTS, dtype=jnp.int32)[:, None]
-    put = (slot[:, None] == jnp.arange(SLOTS, dtype=jnp.int32)[None, :]).astype(BF)
     place = jnp.arange(tok, dtype=jnp.int32)
     ends = jnp.cumsum(lengths)
     starts = jnp.max(jnp.where(ends[None, :] <= seq_at * tok + place[:, None], ends[None, :], 0), axis=1)
     low_of = starts - (seq_at - REACH) * tok
-    low = jnp.sum(jnp.where(pick, low_of[None, :], 0), axis=1)
-    high = jnp.sum(jnp.where(pick, place[None, :], 0), axis=1) + REACH * tok
-    share = jnp.sum(jnp.where(pick, share_of[None, :], 0.0), axis=1)
-    left_share = jnp.tile(share[MAIN:CAP], left_rows // LEFT)
     q_cols = lax.dynamic_slice_in_dim(queries, rep_at * cols, cols, 1)
     q_rows = dot(pick.astype(BF), q_cols).astype(BF)
 
-    spread, share, left_share = call(
+    spread, put, share, left_share = call(
         functools.partial(attend_kernel, heads, kv_heads),
         [
             jax.ShapeDtypeStruct((flat, HD), BF),
+            jax.ShapeDtypeStruct((tok, SLOTS), BF),
             jax.ShapeDtypeStruct((MAIN, 1), F32),
             jax.ShapeDtypeStruct((left_rows, 1), F32),
         ],
         flops=4 * heads * SLOTS * 3 * tok * HD,
-    )(q_rows, far, near, kv, jnp.tile(low, group)[:, None], jnp.tile(high, group)[:, None], share[:MAIN, None], left_share[:, None])
+    )(q_rows, far, near, kv, slot[None], low_of[None], share_of[None])
 
     gate_w = jnp.transpose(gate_up, (0, 2, 3, 1))
     down_w = jnp.transpose(down_t, (0, 2, 1))
     sib_gate_w = lax.ppermute(gate_w, "seq", sibling)
     sib_down_w = lax.ppermute(down_w, "seq", sibling)
     mine = lax.all_gather(spread, "seq", axis_index_groups=same_core)
-    mine, sib_gate_w, sib_down_w, put = lax.optimization_barrier(
-        (mine, sib_gate_w, sib_down_w, put)
-    )
+    mine, sib_gate_w, sib_down_w = lax.optimization_barrier((mine, sib_gate_w, sib_down_w))
 
     full = 2 * hid // HD
     m, n = n_y * MAIN // n_rep, n_y * LEFT // n_rep

time: 137 us -> 136 us (level)
  blocking collectives: 116 us -> 113 us
    all_to_all x1, blocking collectives: 27.5 us -> 23.4 us  [per_device(): lax.all_to_all(term.reshape(n_exp, tok // n_exp, cols), 'exp', split_axis...]
    unnamed x6, local copies, waits for them, and re-layouts: 0.02 us -> 1.59 us
  transfers between devices with their start and end apart: 4 -> 4, of which waited for: 0 -> 1; matrix products, arithmetic and copies ran while one was open for 2% -> 2% of each run, Pallas kernels for 1% -> 1%
where the time goes in v4:
time: 136 us; the launch traced here: 134 us
  blocking collectives  113 us (83%)
  starting transfers between devices  9.08 us (7%)
  Pallas kernels  5.72 us (4%)
  local copies, waits for them, and re-layouts  3.21 us (2%)
  other arithmetic  1.99 us (1%)
    all_gather x1, blocking collectives, per_device(): mine = lax.all_gather(spread, 'seq', axis_index_groups=same_core)  27 us
    all_to_all x1, blocking collectives, per_device(): lax.all_to_all(parts, 'rep', split_axis=0, concat_axis=0, tiled=True)  25.8 us
    all_to_all x1, blocking collectives, per_device(): lax.all_to_all(term.reshape(n_exp, tok // n_exp, cols), 'exp', split_axis...  23.4 us
    all_to_all x1, blocking collectives, per_device(): lax.all_to_all(mine, 'seq', split_axis=0, concat_axis=0, tiled=True, axis...  21.4 us
    all_gather x1, blocking collectives, per_device(): hidden = lax.all_gather(hidden, 'rep')  14.9 us
    ppermute x1, starting transfers between devices, per_device(): far = lax.ppermute(kv, 'seq', [(i, (i + 2) % n_seq) for i in range(n_seq)])  3.59 us
    ppermute x1, starting transfers between devices, per_device(): sib_down_w = lax.ppermute(down_w, 'seq', sibling)  2.94 us
    pallas_call x1, Pallas kernels, per_device(): call(functools.partial(gate_kernel, heads), jax.ShapeDtypeStruct((n_rep,...  2.9 us
  transfers between devices with their start and end apart: 4, of which 1 were waited for; matrix products, arithmetic and copies ran while one was open for 2% of the time, Pallas kernels for 1%

profile of v4, /device:TPU:14, one launch (start us, length us, event | category | flops | bytes accessed | tf_op | source)
XLA Modules:
  0.0 133.9 jit_solution(4309632835078952564)
XLA Ops:
  0.0 2.0 %collective-permute-start.2 = (bf16[1,2,336,1536]{3,2,1,0:T(8,128)(2,1)}, bf16[1,2,336,1536]{3,2,1,0:T(8,128)(2,1)}, u32[]{:S(2)}, u32[]{:S(2)}) collective-permute-start(bf16[1,2,336,1536]{3,2,1,0:T(8,128)(2,1)} %bitcast.18), channel_id=1, source_target_pairs={{0,64},{64,0},{128,192},{192,128},{256,320},{320,256},{384,448},{4... | collective-permute-start | bytes 6193160 | tf_op jit(solution)/shard_map/ppermute | solution.py:306
  2.1 0.9 constant_dynamic-slice_fusion
  3.0 0.5 collective-permute-start.1
  3.5 3.6 %collective-permute-start = (bf16[128,512]{1,0:T(8,128)(2,1)S(1)}, bf16[128,512]{1,0:T(8,128)(2,1)S(1)}, u32[]{:S(2)}, u32[]{:S(2)}) collective-permute-start(bf16[128,512]{1,0:T(8,128)(2,1)S(1)} %pad_maximum_fusion.own_ref), channel_id=1, source_target_pairs={{0,128},{64,192},{128,256},{192,320},{256,384},{320,448},{384,512}... | collective-permute-start | bytes 393224 | tf_op jit(solution)/shard_map/ppermute | solution.py:277
  7.1 2.9 %collective-permute-start.3 = (bf16[1,336,1536]{2,1,0:T(8,128)(2,1)}, bf16[1,336,1536]{2,1,0:T(8,128)(2,1)S(1)}, u32[]{:S(2)}, u32[]{:S(2)}) collective-permute-start(bf16[1,336,1536]{2,1,0:T(8,128)(2,1)} %bitcast.22), channel_id=1, source_target_pairs={{0,64},{64,0},{128,192},{192,128},{256,320},{320,256},{384,448},{4... | collective-permute-start | bytes 3096584 | tf_op jit(solution)/shard_map/ppermute | solution.py:307
  10.0 0.7 select_reduce_fusion.1
  10.8 0.3 reduce-window_clone.1
  11.1 0.7 copy.11
  11.9 0.1 reduce.1
  12.0 0.1 select_reduce_fusion
  12.1 0.2 convolution_convert_fusion.q_ref
  12.3 1.0 collective-permute-done.far_ref
  13.3 1.1 shard_map.82
  14.5 27.0 %all-gather = bf16[3328,128]{1,0:T(8,128)(2,1)S(1)} all-gather(bf16[416,128]{1,0:T(8,128)(2,1)S(1)} %get-tuple-element.12), channel_id=2, replica_groups={{0,128,256,384,512,640,768,896},{64,192,320,448,576,704,832,960},{1,129..., dimensions={0}, use_global_device_ids=true | all-gather | bytes 958464 | tf_op jit(solution)/shard_map/all_gather | solution.py:308
  41.5 1.6 %copy-done.1 = bf16[1,1536,2,336]{1,3,2,0:T(8,128)(2,1)S(1)} copy-done((bf16[1,1536,2,336]{1,3,2,0:T(8,128)(2,1)S(1)}, bf16[1,1536,2,336]{1,3,2,0:T(8,128)(2,1)}, u32[]{:S(2)}) %copy-start.1) | copy-done | bytes 2064408
  43.1 2.9 %shard_map.83 = bf16[4,720,128]{2,1,0:T(8,128)(2,1)S(1)} custom-call(bf16[8,416,128]{2,1,0:T(8,128)(2,1)S(1)} %bitcast.17, bf16[1,2,336,1536]{3,2,1,0:T(8,128)(2,1)S(1)} %bitcast.19, bf16[1,2,336,1536]{3,2,1,0:T(8,128)(2,1)} %collective-permute-done.2.far_w_ref), custom_call_target="tpu_custom_call" | custom-call | flops 1123024896 | tf_op jit(solution)/shard_map/pallas_call | solution.py:315
  46.0 25.8 %all_to_all.15.in_ref = bf16[4,720,128]{2,1,0:T(8,128)(2,1)S(1)} all-to-all(bf16[4,720,128]{2,1,0:T(8,128)(2,1)S(1)} %shard_map.83), channel_id=1, replica_groups=mesh['seq'=16,'exp'=16,'rep'=4] {'rep'}, dimensions={0} | all-to-all | bytes 1474560 | tf_op jit(solution)/shard_map/all_to_all | solution.py:322
  71.8 0.2 shard_map.84
  72.0 14.9 %all-gather.1 = bf16[1536,128]{1,0:T(8,128)(2,1)S(1)} all-gather(bf16[384,128]{1,0:T(8,128)(2,1)S(1)} %shard_map.84), channel_id=3, replica_groups=mesh['seq'=16,'exp'=16,'rep'=4] {'rep'}, dimensions={0}, use_global_device_ids=true | all-gather | bytes 491520 | tf_op jit(solution)/shard_map/all_gather | solution.py:324
  86.9 1.0 shard_map.85
  88.0 21.4 %all_to_all.16.in_ref = bf16[8,416,128]{2,1,0:T(8,128)(2,1)S(1)} all-to-all(bf16[8,416,128]{2,1,0:T(8,128)(2,1)S(1)} %shard_map.85), channel_id=1, replica_groups={{0,128,256,384,512,640,768,896},{64,192,320,448,576,704,832,960},{1,129..., dimensions={0} | all-to-all | bytes 1703936 | tf_op jit(solution)/shard_map/all_to_all | solution.py:330
  109.4 0.4 shard_map.86
  109.8 23.4 %all_to_all.17 = bf16[16,8,1536]{2,1,0:T(8,128)(2,1)S(1)} all-to-all(bf16[16,8,1536]{2,1,0:T(8,128)(2,1)S(1)} %bitcast.21), channel_id=1, replica_groups=mesh['seq'=16,'exp'=16,'rep'=4] {'exp'}, dimensions={0} | all-to-all | bytes 786432 | tf_op jit(solution)/shard_map/all_to_all | solution.py:337
  133.2 0.7 reduce_sum.22
  (16 shorter events, 0.1 us)
Async XLA Ops:
  0.0 12.1 %copy-start = (bf16[128,6144]{1,0:T(8,128)(2,1)S(1)}, bf16[128,6144]{1,0:T(8,128)(2,1)}, u32[]{:S(2)}) copy-start(bf16[128,6144]{1,0:T(8,128)(2,1)} %param.8) | copy-start | bytes 4718596
  0.0 41.5 %collective-permute-start.2 = (bf16[1,2,336,1536]{3,2,1,0:T(8,128)(2,1)}, bf16[1,2,336,1536]{3,2,1,0:T(8,128)(2,1)}, u32[]{:S(2)}, u32[]{:S(2)}) collective-permute-start(bf16[1,2,336,1536]{3,2,1,0:T(8,128)(2,1)} %bitcast.18), channel_id=1, source_target_pairs={{0,64},{64,0},{128,192},{192,128},{256,320},{320,256},{384,448},{4... | collective-permute-start | bytes 6193160 | tf_op jit(solution)/shard_map/ppermute | solution.py:306
  3.0 9.3 %collective-permute-start.1 = (bf16[128,512]{1,0:T(8,128)(2,1)S(1)}, bf16[128,512]{1,0:T(8,128)(2,1)S(1)}, u32[]{:S(2)}, u32[]{:S(2)}) collective-permute-start(bf16[128,512]{1,0:T(8,128)(2,1)S(1)} %pad_maximum_fusion.own_ref), channel_id=1, source_target_pairs={{0,64},{64,128},{128,192},{192,256},{256,320},{320,384},{384,448},... | collective-permute-start | bytes 393224 | tf_op jit(solution)/shard_map/ppermute | solution.py:278
  3.5 9.8 %collective-permute-start = (bf16[128,512]{1,0:T(8,128)(2,1)S(1)}, bf16[128,512]{1,0:T(8,128)(2,1)S(1)}, u32[]{:S(2)}, u32[]{:S(2)}) collective-permute-start(bf16[128,512]{1,0:T(8,128)(2,1)S(1)} %pad_maximum_fusion.own_ref), channel_id=1, source_target_pairs={{0,128},{64,192},{128,256},{192,320},{256,384},{320,448},{384,512}... | collective-permute-start | bytes 393224 | tf_op jit(solution)/shard_map/ppermute | solution.py:277
  7.1 34.4 %collective-permute-start.3 = (bf16[1,336,1536]{2,1,0:T(8,128)(2,1)}, bf16[1,336,1536]{2,1,0:T(8,128)(2,1)S(1)}, u32[]{:S(2)}, u32[]{:S(2)}) collective-permute-start(bf16[1,336,1536]{2,1,0:T(8,128)(2,1)} %bitcast.22), channel_id=1, source_target_pairs={{0,64},{64,0},{128,192},{192,128},{256,320},{320,256},{384,448},{4... | collective-permute-start | bytes 3096584 | tf_op jit(solution)/shard_map/ppermute | solution.py:307
  41.5 1.6 %copy-start.1 = (bf16[1,1536,2,336]{1,3,2,0:T(8,128)(2,1)S(1)}, bf16[1,1536,2,336]{1,3,2,0:T(8,128)(2,1)}, u32[]{:S(2)}) copy-start(bf16[1,1536,2,336]{1,3,2,0:T(8,128)(2,1)} %param.14) | copy-start | bytes 6193156
  46.0 41.0 %copy-start.2 = (bf16[1,1536,336]{1,2,0:T(8,128)(2,1)S(1)}, bf16[1,1536,336]{1,2,0:T(8,128)(2,1)}, u32[]{:S(2)}) copy-start(bf16[1,1536,336]{1,2,0:T(8,128)(2,1)} %param.15) | copy-start | bytes 3096580
